TPU v7x, 256 devices: a whole 4x4x8 slice. The times are simulated.
256 devices in a mesh: frames: 64 (over x, y, z_lo, core), chan: 4 (over z_hi).
Axes of the slice: x: 4, y: 4, z: 8 (z_hi: 4, z_lo: 2; z = z_hi * 2 + z_lo), core: 2. Of those that a mesh axis runs over, the one named last changes fastest.
Arguments:
- inputs: bfloat16 [128, 256, 16, 128], P('frames', 'chan'), may hold values from -6 to 6
- saved: bfloat16 [128, 256, 16, 128], P('frames', 'chan'), may hold values from -6 to 6
- cotangent: bfloat16 [64, 256, 512], P('frames', 'chan'), may hold values from -24 to 24
- spatial_w: bfloat16 [3, 3, 256, 256], P(None, None, 'chan'), may hold values from -0.125 to 0.125
- temporal_w: bfloat16 [3, 256, 256], replicated, may hold values from -0.21875 to 0.21875
Outputs:
- input_grad: bfloat16 [128, 256, 16, 128], P('frames', 'chan')
- spatial_grad: float32 [3, 3, 256, 256], P(None, None, 'chan')
- temporal_grad: float32 [3, 256, 256], P(None, 'chan')
All inputs are finite; a program needn't handle non-finite values.
Results may differ from a plain program's by a relative error of at most 0.0049.
Values may be sent and summed in bfloat16 or wider, within the bound.
A program may use at most 64 MiB of HBM per device.

v0:
```python
import math

import jax
import jax.numpy as jnp
from jax import lax
from jax.sharding import PartitionSpec as P


def padded(cells, sides, width):
    for axis, dim in sides:
        count = lax.axis_size(axis)
        ends = count - 1
        head = lax.slice_in_dim(cells, 0, width, axis=dim)
        tail = lax.slice_in_dim(cells, cells.shape[dim] - width, cells.shape[dim], axis=dim)
        cells = jnp.concatenate(
            [
                lax.ppermute(tail, axis, [(i, (i + 1) % count) for i in range(ends)]),
                cells,
                lax.ppermute(head, axis, [((i + 1) % count, i) for i in range(ends)]),
            ],
            axis=dim,
        )
    return cells


def upsample_pairs(pooled, row_half, col_half):
    frame_total, channels = (pooled.shape[0], pooled.shape[1])
    blocks = pooled.reshape(frame_total, 1, channels, row_half, 1, col_half, 1)
    blocks = jnp.broadcast_to(blocks, (frame_total, 2, channels, row_half, 2, col_half, 2))
    return blocks.reshape(frame_total * 2, channels, row_half * 2, col_half * 2)


def temporal_terms(saved_ext, grad_ext, temporal_w, row_total, frame_count):
    result = jnp.zeros((frame_count, row_total, grad_ext.shape[2]), jnp.float32)
    for tap in range(3):
        result = result + jnp.einsum(
            "fol,io->fil",
            grad_ext[2 - tap : 2 - tap + frame_count],
            temporal_w[tap],
            preferred_element_type=jnp.float32,
        )
    partial_value = jnp.stack(
        [
            jnp.einsum(
                "fil,fol->io",
                saved_ext[tap : tap + frame_count],
                grad_ext[1 : frame_count + 1],
                preferred_element_type=jnp.float32,
            )
            for tap in range(3)
        ]
    )
    return (result.astype(jnp.bfloat16), partial_value)


def shards(inputs, saved, cotangent, spatial_w, temporal_w):
    frame_count, quarter, row_count, col_count = inputs.shape
    channels = temporal_w.shape[1]
    row_half, col_half = (row_count // 2, col_count // 2)
    scale = 1.0 / math.sqrt(frame_count * lax.axis_size("frames") * row_count * col_count)
    full_cot = lax.all_gather(cotangent, "chan", axis=1, tiled=True)
    row_first, row_total = (0, channels)
    saved_ext = padded(saved, (("frames", 0),), 1)
    cot_ext = padded(full_cot, (("frames", 0),), 1)
    spread = upsample_pairs(cot_ext.reshape(3, channels, row_half, col_half), row_half, col_half)
    upsampled = (spread[1 : frame_count + 3].astype(jnp.float32) * 0.125).astype(jnp.bfloat16)
    cell_total = row_count * col_count
    grad_ext = upsampled.reshape(frame_count + 2, channels, cell_total)
    saved_flat = saved_ext.reshape(frame_count + 2, quarter, cell_total)
    flat_grad, temporal_part = temporal_terms(
        saved_flat, grad_ext, temporal_w, row_total, frame_count
    )
    saved_grad = flat_grad.reshape(frame_count, row_total, row_count, col_count)
    temporal_total = lax.psum(temporal_part, "frames")
    space_pad = ((0, 0), (0, 0), (1, 1), (1, 1))
    grad_pad = jnp.pad(saved_grad, space_pad)
    input_pad = jnp.pad(inputs, space_pad)
    input_sum = jnp.zeros((frame_count, quarter, row_count, col_count), jnp.float32)
    kernel_rows = []
    for tap_row in range(3):
        kernel_cols = []
        for tap_col in range(3):
            window = grad_pad[
                :, :, 2 - tap_row : 2 - tap_row + row_count, 2 - tap_col : 2 - tap_col + col_count
            ]
            input_sum = input_sum + jnp.einsum(
                "fohw,io->fihw",
                window,
                spatial_w[tap_row, tap_col],
                preferred_element_type=jnp.float32,
            )
            shifted = input_pad[:, :, tap_row : tap_row + row_count, tap_col : tap_col + col_count]
            kernel_cols.append(
                jnp.einsum("fihw,fohw->io", shifted, saved_grad, preferred_element_type=jnp.float32)
            )
        kernel_rows.append(jnp.stack(kernel_cols))
    spatial_part = jnp.stack(kernel_rows)
    spatial_total = lax.psum(spatial_part, "frames")
    return (input_sum.astype(jnp.bfloat16), spatial_total * scale, temporal_total * scale)


def solution(mesh):
    return jax.shard_map(
        shards,
        mesh=mesh,
        in_specs=(
            P("frames", "chan", None, None),
            P("frames", "chan", None, None),
            P("frames", "chan", None),
            P(None, None, "chan", None),
            P(),
        ),
        out_specs=(
            P("frames", "chan", None, None),
            P(None, None, "chan", None),
            P(None, "chan", None),
        ),
        check_vma=False,
    )
```

profile of v0, /device:TPU:1, one launch (start us, length us, event | category | flops | bytes accessed | tf_op | source)
XLA Modules:
  0.0 651.9 jit_solution(18174378903664320921)
XLA Ops:
  7.2 16.6 %all_gather.3 = bf16[1,256,512]{2,1,0:T(8,128)(2,1)S(1)} all-gather(bf16[1,64,512]{2,1,0:T(8,128)(2,1)} %param.7), channel_id=1, replica_groups=mesh['frames'=64,'chan'=4] {'chan'}, dimensions={1}, use_global_device_ids=true | all-gather | bytes 327680 | tf_op jit(solution)/shard_map/all_gather | solution.py:61
  24.0 5.0 collective-permute-start.1
  29.0 2.5 collective-permute-start
  31.6 1.2 copy.75
  32.8 0.8 fusion.74
  33.6 2.4 collective-permute-start.2
  36.0 2.6 collective-permute-start.3
  38.9 4.3 broadcast_in_dim.8
  43.2 10.2 %reshape.21 = bf16[6,256,16,128]{1,3,2,0:T(8,128)(2,1)} reshape(bf16[3,2,256,8,2,64,2]{2,6,5,4,3,1,0:T(2,128)(2,1)} %broadcast_in_dim.8) | data formatting | bytes 12582912 | tf_op jit(solution)/shard_map/reshape | solution.py:30
  53.4 4.7 slice.167
  58.1 6.3 copy.112
  64.4 3.0 convolution_bitcast_fusion.1
  67.3 3.7 multiply_convert_fusion
  71.1 3.6 fusion.73
  74.6 2.6 copy.61
  77.3 2.9 copy.60
  80.2 4.0 copy.59
  84.2 0.7 fusion.25
  84.9 0.8 copy-done.5
  85.8 0.7 fusion.27
  86.5 0.9 copy-done.4
  87.4 0.7 add_convert_fusion
  88.1 1.1 convolution_bitcast_fusion.4
  89.3 1.1 convolution_bitcast_fusion.5
  90.4 1.1 convolution_bitcast_fusion.6
  91.5 0.5 convolution_bitcast_fusion.7
  92.0 1.1 convolution_bitcast_fusion.3
  93.1 1.1 convolution_bitcast_fusion.8
  94.2 1.1 convolution_bitcast_fusion.9
  95.3 2.4 copy.62
  97.7 0.7 fusion.36
  98.5 0.8 copy-done
  99.3 0.7 fusion
  100.5 0.8 fusion.14
  101.3 0.9 fusion.13
  102.2 1.8 fusion.11
  104.5 0.5 convolution_bitcast_fusion.11
  105.0 1.2 copy-done.3
  106.2 1.7 convolution_bitcast_fusion.2
  108.0 1.8 convolution_bitcast_fusion
  109.8 0.7 pad_maximum_fusion.2
  110.6 0.9 pad_maximum_fusion.1
  111.9 0.8 fusion.10
  113.2 0.8 fusion.17
  114.0 1.1 copy.80
  115.1 526.4 %all-reduce.5.cloned.1.call-done = (f32[3,3,64,256]{3,2,1,0:T(8,128)}, f32[3,64,256]{2,1,0:T(8,128)}) async-done(((f32[3,3,64,256]{3,2,1,0:T(8,128)}, f32[3,64,256]{2,1,0:T(8,128)}), (f32[3,3,64,256]{3,2,1,0:T(8,128)}, f32[3,64,256]{2,1,0:T(8,128)})) %all-reduce.5.cloned.1.call-update) | async-done | bytes 786448 | tf_op jit(solution)/shard_map/psum | solution.py:98
  641.5 1.9 broadcast_multiply_fusion
  643.4 1.6 broadcast_multiply_fusion.1
  (48 shorter events, 2.4 us)
Async XLA Ops:
  7.2 31.5 %copy-start.7 = (bf16[2,64,16,128]{3,2,1,0:T(8,128)(2,1)S(1)}, bf16[2,64,16,128]{3,2,1,0:T(8,128)(2,1)}, u32[]{:S(2)}) copy-start(bf16[2,64,16,128]{3,2,1,0:T(8,128)(2,1)} %param.5) | copy-start | bytes 1572868
  7.2 634.3 %all-reduce.5.cloned.1.call-start = ((), (), s32[]{:S(2)}) async-start(), calls=%async_computation | async-start | bytes 1572864 | tf_op jit(solution)/shard_map/psum | solution.py:98
  24.0 14.8 %collective-permute-start.1 = (bf16[1,256,512]{1,2,0:T(8,128)(2,1)S(1)}, bf16[1,256,512]{1,2,0:T(8,128)(2,1)S(1)}, u32[]{:S(2)}, u32[]{:S(2)}) collective-permute-start(bf16[1,256,512]{1,2,0:T(8,128)(2,1)S(1)} %copy.55), channel_id=1, source_target_pairs={{4,0},{8,4},{12,8},{16,12},{20,16},{24,20},{28,24},{32,28},{36,32}... | collective-permute-start | bytes 786440 | tf_op jit(solution)/shard_map/ppermute | solution.py:19
  29.0 9.8 %collective-permute-start = (bf16[1,256,512]{1,2,0:T(8,128)(2,1)S(1)}, bf16[1,256,512]{1,2,0:T(8,128)(2,1)S(1)}, u32[]{:S(2)}, u32[]{:S(2)}) collective-permute-start(bf16[1,256,512]{1,2,0:T(8,128)(2,1)S(1)} %copy.55), channel_id=1, source_target_pairs={{0,4},{4,8},{8,12},{12,16},{16,20},{20,24},{24,28},{28,32},{32,36}... | collective-permute-start | bytes 786440 | tf_op jit(solution)/shard_map/ppermute | solution.py:17
  33.6 71.4 %collective-permute-start.2 = (bf16[1,64,16,128]{3,1,2,0:T(8,128)(2,1)}, bf16[1,64,16,128]{3,1,2,0:T(8,128)(2,1)}, u32[]{:S(2)}, u32[]{:S(2)}) collective-permute-start(bf16[1,64,16,128]{3,1,2,0:T(8,128)(2,1)} %get-tuple-element.17), channel_id=1, source_target_pairs={{0,4},{4,8},{8,12},{12,16},{16,20},{20,24},{24,28},{28,32},{32,36}... | collective-permute-start | bytes 786440 | tf_op jit(solution)/shard_map/ppermute | solution.py:17
  36.0 71.9 %collective-permute-start.3 = (bf16[1,64,16,128]{3,1,2,0:T(8,128)(2,1)}, bf16[1,64,16,128]{3,1,2,0:T(8,128)(2,1)}, u32[]{:S(2)}, u32[]{:S(2)}) collective-permute-start(bf16[1,64,16,128]{3,1,2,0:T(8,128)(2,1)} %get-tuple-element.18), channel_id=1, source_target_pairs={{4,0},{8,4},{12,8},{16,12},{20,16},{24,20},{28,24},{32,28},{36,32}... | collective-permute-start | bytes 786440 | tf_op jit(solution)/shard_map/ppermute | solution.py:19
  58.1 6.3 copy-start.9
  71.1 3.6 copy-start.2
  80.1 4.0 copy-start.10
  84.2 1.6 copy-start.5
  85.8 1.6 copy-start.4
  90.3 1.6 copy-start.8
  95.3 2.4 copy-start.11
  97.7 1.6 copy-start
  104.0 2.2 copy-start.3
  107.9 1.9 copy-start.18
  107.9 2.6 copy-start.15
  107.9 2.6 copy-start.16
  107.9 2.6 copy-start.17
  107.9 2.6 copy-start.12
  107.9 2.6 copy-start.13
  107.9 2.6 copy-start.14
  109.8 1.7 copy-start.1
  109.8 2.1 copy-start.6
Sparse Core Ops, SparseCore 0:
  111.6 529.8 all-reduce.4
where the time goes:
time: 654 us; the launch traced here: 652 us
  waiting for transfers between devices  526 us (80%)
  local copies, waits for them, and re-layouts  48.6 us (7%)
  matrix products  24.3 us (4%)
  blocking collectives  16.6 us (3%)
  between operations  14.4 us (2%)
  starting transfers between devices  12.6 us (2%)
  other arithmetic  8.93 us (1%)
    psum x1, waiting for transfers between devices, shards(): spatial_total = lax.psum(spatial_part, 'frames')  526 us
    all_gather x1, blocking collectives, shards(): full_cot = lax.all_gather(cotangent, 'chan', axis=1, tiled=True)  16.6 us
    slice x4, local copies, waits for them, and re-layouts, temporal_terms(): grad_ext[2 - tap:2 - tap + frame_count]  13.1 us
  transfers between devices with their start and end apart: 5, of which 1 were waited for; matrix products, arithmetic and copies ran while one was open for 11% of the time, Pallas kernels for 0%

commit v1 on v0

v1 whole, which is shorter than its diff:
```python
import math

import jax
import jax.numpy as jnp
from jax import lax
from jax.experimental import pallas as pl
from jax.experimental.pallas import tpu as pltpu
from jax.sharding import PartitionSpec as P

BF = jnp.bfloat16
F32 = jnp.float32
CHIPS = 32
UNITS = 24


def dot(a, b):
    return jnp.dot(a, b, preferred_element_type=F32)


def dot_nt(a, b):
    return lax.dot_general(a, b, (((1,), (1,)), ((), ())), preferred_element_type=F32)


def kernel(
    x_h, s_h, c_h, sw_h, tw_h,
    ig_h, gr_v,
    x_v, s_v, sw_v, tw_v, ring, halo, pool, q_v, sq_v, a_v, g_v, p_v, xe_v, z_v, out_v,
    partf, part, xch, half_v, rs_v,
    load_sem, ring_send, ring_recv, fwd_send, halo_recv,
    xch_send, xch_recv, rs_send, rs_recv, ag_send, ag_recv, sib_send, sib_recv, out_sem,
):
    p = lax.axis_index("frames")
    c = lax.axis_index("chan")
    core = lax.rem(p, 2)
    chip = lax.div(p, 2)
    zl = lax.rem(chip, 2)
    column = lax.div(chip, 2)
    z = 2 * c + zl

    def at_z(zz):
        zz = lax.rem(zz, 8)
        return (4 * column + 2 * lax.rem(zz, 2) + core, lax.div(zz, 2))

    up, down = at_z(z + 1), at_z(z + 7)
    sibling = (p + 1 - 2 * core, c)
    differ = jnp.where(zl == core, 0, 1)
    to_step = jnp.where(zl == core, 1 - 2 * core, jnp.where(core == 1, 3, -3))
    from_step = jnp.where(zl == core, jnp.where(core == 0, -3, 3), jnp.where(core == 1, -1, 1))
    to_frame, from_frame = p + to_step, p + from_step
    last = 4 * 16
    to_ok = jnp.logical_and(to_frame >= 0, to_frame < last)
    from_ok = jnp.logical_and(from_frame >= 0, from_frame < last)

    barrier = pltpu.get_barrier_semaphore()

    def greet(device):
        pl.semaphore_signal(barrier, inc=1, device_id=device, device_id_type=pl.DeviceIdType.MESH)

    greet(up)
    greet(down)
    greet(sibling)

    @pl.when(to_ok)
    def _():
        greet((to_frame, c))

    @pl.when(from_ok)
    def _():
        greet((from_frame, c))

    def greet_chip(j, carry):
        greet((2 * lax.rem(chip + j, CHIPS) + core, c))
        return carry

    lax.fori_loop(1, CHIPS, greet_chip, 0)

    loads = [
        pltpu.make_async_copy(c_h.at[0], ring.at[0, c], load_sem.at[0]),
        pltpu.make_async_copy(s_h, s_v, load_sem.at[1]),
        pltpu.make_async_copy(x_h, x_v, load_sem.at[2]),
        pltpu.make_async_copy(tw_h, tw_v, load_sem.at[3]),
        pltpu.make_async_copy(sw_h, sw_v, load_sem.at[4]),
    ]
    for load in loads:
        load.start()

    pl.semaphore_wait(
        barrier, 34 + jnp.where(to_ok, 1, 0) + jnp.where(from_ok, 1, 0)
    )

    def remote(src, dst, send, recv, device):
        return pltpu.make_async_remote_copy(
            src_ref=src, dst_ref=dst, send_sem=send, recv_sem=recv,
            device_id=device, device_id_type=pl.DeviceIdType.MESH,
        )

    sent = []

    def rows(half):
        return pl.ds(32 * half, 32)

    def ring_send_step(way, step, half):
        zz = z + (8 - step if way == 0 else step)
        quarter = lax.div(lax.rem(zz, 8), 2)
        if step == 0:
            src = c_h.at[0, rows(half)]
        else:
            src = ring.at[step % 2, quarter, rows(half)]
        copy = remote(
            src, ring.at[(step + 1) % 2, quarter, rows(half)],
            ring_send.at[way, step, half], ring_recv.at[way, step, half],
            up if way == 0 else down,
        )
        copy.start()
        sent.append(copy)

    def ring_wait_step(way, step, half):
        zz = z + (7 - step if way == 0 else 1 + step)
        quarter = lax.div(lax.rem(zz, 8), 2)
        dst = ring.at[(step + 1) % 2, quarter, rows(half)]
        remote(
            dst, dst, ring_send.at[way, step, half], ring_recv.at[way, step, half],
            down if way == 0 else up,
        ).wait_recv()
        return quarter

    def forward_own(src, quarter, index):
        copy = remote(src, halo.at[core, quarter], fwd_send.at[index], halo_recv.at[0], sibling)
        copy.start()
        sent.append(copy)

    def forward_other(quarter, index):
        copy = remote(
            ring.at[1, quarter], halo.at[1 - core, quarter],
            fwd_send.at[index], halo_recv.at[1], (to_frame, c),
        )

        @pl.when(to_ok)
        def _():
            copy.start()

        return copy

    for half in range(2):
        ring_send_step(0, 0, half)
        ring_send_step(1, 0, half)
    forward_own(c_h.at[0], c, 0)

    lane = lax.broadcasted_iota(jnp.int32, (128, 384), 1)
    column_of = lax.broadcasted_iota(jnp.int32, (128, 384), 0)
    first = 2 * (lane & 63) + (lane >> 7) - 1
    pairs = jnp.where(
        jnp.logical_or(column_of == first, column_of == first + 1), 1.0, 0.0
    ).astype(BF)
    low = lax.broadcasted_iota(jnp.int32, (64, 128), 1) < 64

    loads[1].wait()
    for f in range(2):
        pool[0, pl.ds(f * 1024, 1024), :] = dot(
            s_v[f].reshape(1024, 128), pairs[:, 128:256]
        )
        height = [pool[0, pl.ds(f * 1024 + h, 64, stride=16), :] for h in range(16)]
        for j in range(4):
            upper = height[4 * j] + height[4 * j + 1]
            lower = height[4 * j + 2] + height[4 * j + 3]
            sq_v[pl.ds(64 * f, 64), 128 * j : 128 * j + 128] = jnp.where(low, upper, lower).astype(BF)

    others = []

    def ring_step(step):
        for way in range(2):
            for half in range(2):
                if step == 3 and half != way:
                    continue
                quarter = ring_wait_step(way, step, half)
                if step < 2 or (step == 2 and half == way):
                    ring_send_step(way, step + 1, half)
            if step == 0 or step == 2:
                others.append(forward_other(quarter, 4 + step + way))
            elif step == 1:
                forward_own(ring.at[0, quarter], quarter, 1 + way)
        if step == 3:
            forward_own(ring.at[0, quarter], quarter, 3)

    ring_step(0)
    loads[2].wait()
    for f in range(2):
        sums = dot(x_v[f].reshape(1024, 128), pairs)
        for b in range(3):
            pool[1 + b, pl.ds(f * 1024, 1024), :] = sums[:, 128 * b : 128 * b + 128]
    ring_step(1)
    for f in range(2):
        for b in range(3):
            height = [pool[1 + b, pl.ds(f * 1024 + h, 64, stride=16), :] for h in range(16)]
            total = (
                [height[0]] + [height[h] + height[h + 1] for h in range(15)] + [height[15]]
            )
            for a in range(3):
                for j in range(4):
                    q_v[f, pl.ds((3 * a + b) * 64, 64), 128 * j : 128 * j + 128] = jnp.where(
                        low, total[4 * j + a], total[4 * j + a + 2]
                    ).astype(BF)
        if f == 0:
            ring_step(2)
    loads[0].wait()
    loads[3].wait()
    ring_step(3)

    own = ring[0].reshape(256, 512)
    a_v[...] = dot(tw_v[...].reshape(768, 256), own)
    t_own = dot_nt(sq_v[...], own)

    dst = halo.at[1 - core]
    pltpu.make_async_copy(dst, dst, halo_recv.at[0]).wait()

    @pl.when(from_ok)
    def _():
        dst = halo.at[core]
        pltpu.make_async_copy(dst, dst, halo_recv.at[1]).wait()

    @pl.when(jnp.logical_not(from_ok))
    def _():
        halo[core] = jnp.zeros((4, 64, 512), BF)

    before = halo[0].reshape(256, 512)
    after = halo[1].reshape(256, 512)
    middle = a_v[256:512]
    g_v[0] = ((a_v[0:256] + middle + dot(tw_v[2], before)) * 0.125).astype(BF)
    g_v[1] = ((dot(tw_v[0], after) + middle + a_v[512:768]) * 0.125).astype(BF)

    t_after = dot_nt(sq_v[64:128], after)
    t_before = dot_nt(sq_v[0:64], before)
    temporal = [
        (t_own[0:64] + t_after) * 0.125,
        (t_own[0:64] + t_own[64:128]) * 0.125,
        (t_own[64:128] + t_before) * 0.125,
    ]
    for k in range(3):
        partf[4 * k : 4 * k + 4] = temporal[k].reshape(4, 16, 256)
    spatial = dot_nt(q_v[0], g_v[0]) + dot_nt(q_v[1], g_v[1])
    partf[12:48] = spatial.reshape(36, 16, 256)
    part[...] = partf[...].astype(BF)

    mine = pl.ds(core * UNITS, UNITS)
    theirs = pl.ds((1 - core) * UNITS, UNITS)
    exchange = remote(part.at[theirs], xch, xch_send, xch_recv, sibling)
    exchange.start()

    def input_products(f):
        p_v[...] = dot(sw_v[...].reshape(576, 256), g_v[f]).reshape(9, 64, 512)

    cell = lax.broadcasted_iota(jnp.int32, (16, 512), 1)

    def input_parities(f):
        def tile(i, carry):
            here = pl.ds(pl.multiple_of(16 * i, 16), 16)
            tops, bottoms = [], []
            for b in range(3):
                t0, t1, t2 = p_v[b, here, :], p_v[3 + b, here, :], p_v[6 + b, here, :]
                tops.append(t0 + t1 + jnp.where(cell >= 64, pltpu.roll(t2, 64, 1), 0.0))
                bottoms.append(t1 + t2 + jnp.where(cell < 448, pltpu.roll(t0, 448, 1), 0.0))
            for r, (u0, u1, u2) in enumerate((tops, bottoms)):
                even = u0 + u1 + jnp.where((cell & 63) != 0, pltpu.roll(u2, 1, 1), 0.0)
                odd = u1 + u2 + jnp.where((cell & 63) != 63, pltpu.roll(u0, 511, 1), 0.0)
                for j in range(4):
                    cut = slice(128 * j, 128 * j + 128)
                    xe_v[r, j, here, 0:128] = even[:, cut].astype(BF)
                    xe_v[r, j, here, 128:256] = odd[:, cut].astype(BF)
            return carry

        lax.fori_loop(0, 4, tile, 0)

    k_of = lax.broadcasted_iota(jnp.int32, (256, 256), 0)
    w_of = lax.broadcasted_iota(jnp.int32, (256, 256), 1)
    place = ((k_of >> 6) & 1) * 128 + 2 * (k_of & 63) + (k_of >> 7)
    weave = jnp.where(w_of == place, 1.0, 0.0).astype(BF)

    def input_output(f):
        woven = dot(xe_v[...].reshape(512, 256), weave).reshape(2, 4, 64, 256)
        for r in range(2):
            for j in range(4):
                for k in range(2):
                    h = 2 * (2 * j + k) + r
                    z_v[pl.ds(h, 64, stride=16), :] = woven[r, j, :, 128 * k : 128 * k + 128]
        out_v[f] = z_v[...].reshape(64, 16, 128).astype(BF)
        copy = pltpu.make_async_copy(out_v.at[f], ig_h.at[f], out_sem.at[f])
        copy.start()
        return copy

    loads[4].wait()
    input_products(0)

    exchange.wait_recv()
    half_v[...] = (partf[mine] + xch[...].astype(F32)).astype(BF)

    def owner_loop(body):
        def group(g, carry):
            for r in range(3):
                body(3 * g + r, 4 * g + r + core)
            return carry

        lax.fori_loop(0, 8, group, 0)

    def scatter(unit, owner):
        @pl.when(owner != chip)
        def _():
            slot = lax.rem(chip - owner + 63, CHIPS)
            remote(
                half_v.at[unit], rs_v.at[slot], rs_send, rs_recv, (2 * owner + core, c)
            ).start()

    owner_loop(scatter)

    place_in_group = lax.rem(chip, 4) - core
    is_owner = jnp.logical_and(place_in_group >= 0, place_in_group < 3)
    my_unit = 3 * lax.div(chip, 4) + place_in_group

    input_parities(0)
    out_copies = [input_output(0)]

    @pl.when(is_owner)
    def _():
        dst = rs_v.at[pl.ds(0, CHIPS - 1)]
        pltpu.make_async_copy(dst, dst, rs_recv).wait()
        total = half_v[my_unit].astype(F32)
        for slot in range(CHIPS - 1):
            total = total + rs_v[slot].astype(F32)
        gr_v[core * UNITS + my_unit] = total.astype(BF)

        def spread(j, carry):
            src = gr_v.at[core * UNITS + my_unit]
            device = (2 * lax.rem(chip + j, CHIPS) + core, c)
            remote(src, src, ag_send, ag_recv, device).start()
            return carry

        lax.fori_loop(1, CHIPS, spread, 0)

    input_products(1)
    input_parities(1)
    out_copies.append(input_output(1))

    @pl.when(is_owner)
    def _():
        dst = gr_v.at[pl.ds(0, UNITS - 1)]
        pltpu.make_async_copy(dst, dst, ag_recv).wait()

    @pl.when(jnp.logical_not(is_owner))
    def _():
        dst = gr_v.at[pl.ds(0, UNITS)]
        pltpu.make_async_copy(dst, dst, ag_recv).wait()

    handover = remote(gr_v.at[mine], gr_v.at[mine], sib_send, sib_recv, sibling)
    handover.start()

    for copy in sent:
        copy.wait_send()

    @pl.when(to_ok)
    def _():
        for copy in others:
            copy.wait_send()

    exchange.wait_send()

    @pl.when(is_owner)
    def _():
        src = half_v.at[pl.ds(0, UNITS - 1)]
        pltpu.make_async_copy(src, src, rs_send).wait()
        src = rs_v.at[pl.ds(0, CHIPS - 1)]
        pltpu.make_async_copy(src, src, ag_send).wait()

    @pl.when(jnp.logical_not(is_owner))
    def _():
        src = half_v.at[pl.ds(0, UNITS)]
        pltpu.make_async_copy(src, src, rs_send).wait()

    for copy in out_copies:
        copy.wait()
    handover.wait()


def shards(inputs, saved, cotangent, spatial_w, temporal_w):
    scale = 1.0 / math.sqrt(128 * 16 * 128)
    vmem = pltpu.VMEM
    dma = pltpu.SemaphoreType.DMA
    input_grad, grads = pl.pallas_call(
        kernel,
        out_shape=(
            jax.ShapeDtypeStruct((2, 64, 16, 128), BF),
            jax.ShapeDtypeStruct((2 * UNITS, 16, 256), BF),
        ),
        in_specs=[pl.BlockSpec(memory_space=pl.ANY)] * 5,
        out_specs=(
            pl.BlockSpec(memory_space=pl.ANY),
            pl.BlockSpec(memory_space=pltpu.VMEM),
        ),
        scratch_shapes=[
            vmem((2, 64, 16, 128), BF),
            vmem((2, 64, 16, 128), BF),
            vmem((3, 3, 64, 256), BF),
            vmem((3, 256, 256), BF),
            vmem((2, 4, 64, 512), BF),
            vmem((2, 4, 64, 512), BF),
            vmem((4, 2048, 128), F32),
            vmem((2, 576, 512), BF),
            vmem((128, 512), BF),
            vmem((768, 512), F32),
            vmem((2, 256, 512), BF),
            vmem((9, 64, 512), F32),
            vmem((2, 4, 64, 256), BF),
            vmem((1024, 128), F32),
            vmem((2, 64, 16, 128), BF),
            vmem((2 * UNITS, 16, 256), F32),
            vmem((2 * UNITS, 16, 256), BF),
            vmem((UNITS, 16, 256), BF),
            vmem((UNITS, 16, 256), BF),
            vmem((CHIPS - 1, 16, 256), BF),
            dma((5,)),
            dma((2, 4, 2)),
            dma((2, 4, 2)),
            dma((8,)),
            dma((2,)),
            dma, dma,
            dma, dma,
            dma, dma,
            dma, dma,
            dma((2,)),
        ],
        compiler_params=pltpu.CompilerParams(
            collective_id=0, has_side_effects=True, vmem_limit_bytes=56 * 1024 * 1024
        ),
        name="space_time_backward",
    )(inputs, saved, cotangent, spatial_w, temporal_w)
    grads = grads.reshape(12, 64, 256).astype(F32) * scale
    return (input_grad, grads[3:].reshape(3, 3, 64, 256), grads[:3])


def solution(mesh):
    return jax.shard_map(
        shards,
        mesh=mesh,
        in_specs=(
            P("frames", "chan", None, None),
            P("frames", "chan", None, None),
            P("frames", "chan", None),
            P(None, None, "chan", None),
            P(),
        ),
        out_specs=(
            P("frames", "chan", None, None),
            P(None, None, "chan", None),
            P(None, "chan", None),
        ),
        check_vma=False,
    )
```

time: 654 us -> 47.4 us (0.07)
  waiting for transfers between devices: 526 us -> 0 us
  local copies, waits for them, and re-layouts: 48.6 us -> 2.74 us
  Pallas kernels: 0 us -> 42.8 us
  matrix products: 24.3 us -> 0 us
  blocking collectives: 16.6 us -> 0 us
  between operations: 14.4 us -> 0.65 us
  starting transfers between devices: 12.6 us -> 0 us
  other arithmetic: 8.93 us -> 1.08 us
    psum x1 -> x0, waiting for transfers between devices: 526 us -> none  [shards(): spatial_total = lax.psum(spatial_part, 'frames')]
    pallas_call x0 -> x1, Pallas kernels: none -> 42.8 us  [shards(): pl.pallas_call(kernel, out_shape=(jax.ShapeDtypeStruct((2, 64, 16, 128),...]
    dot_general x24 -> x0, matrix products: 24.3 us -> none  [the longest x9 8.17 us: shards(): jnp.einsum('fihw,fohw->io', shifted, saved_grad, preferred_element_type=j...]
    slice x6 -> x2, local copies, waits for them, and re-layouts: 18.7 us -> 1.55 us  [shards(): return (input_grad, grads[3:].reshape(3, 3, 64, 256), grads[:3])]
    all_gather x1 -> x0, blocking collectives: 16.6 us -> none  [shards(): full_cot = lax.all_gather(cotangent, 'chan', axis=1, tiled=True)]
    ppermute x4 -> x0, starting transfers between devices: 12.6 us -> none  [the longest x2 7.65 us: padded(): lax.ppermute(head, axis, [((i + 1) % count, i) for i in range(ends)])]
    reshape x2 -> x0, local copies, waits for them, and re-layouts: 12.6 us -> none  [the longest x1 10.2 us: upsample_pairs(): return blocks.reshape(frame_total * 2, channels, row_half * 2, col_half * 2)]
    unnamed x42 -> x3, local copies, waits for them, and re-layouts: 12.9 us -> 1.19 us
  transfers between devices with their start and end apart: 5 -> 0, of which waited for: 1 -> 0; matrix products, arithmetic and copies ran while one was open for 11% -> 0% of each run, Pallas kernels for 0% -> 0%
where the time goes in v1:
time: 47.4 us; the launch traced here: 47.3 us
  Pallas kernels  42.8 us (90%)
  local copies, waits for them, and re-layouts  2.74 us (6%)
  other arithmetic  1.08 us (2%)
  between operations  0.65 us (1%)
    pallas_call x1, Pallas kernels, shards(): pl.pallas_call(kernel, out_shape=(jax.ShapeDtypeStruct((2, 64, 16, 128),...  42.8 us
    slice x2, local copies, waits for them, and re-layouts, shards(): return (input_grad, grads[3:].reshape(3, 3, 64, 256), grads[:3])  1.55 us
    unnamed x3, local copies, waits for them, and re-layouts  1.19 us
    mul x1, other arithmetic, shards(): grads = grads.reshape(12, 64, 256).astype(F32) * scale  1.08 us

profile of v1, /device:TPU:1, one launch (start us, length us, event | category | flops | bytes accessed | tf_op | source)
XLA Modules:
  0.0 47.3 jit_solution(12271741115320495855)
XLA Ops:
  0.6 42.8 %space_time_backward.1 = (bf16[2,64,16,128]{3,2,1,0:T(8,128)(2,1)}, bf16[48,16,256]{2,1,0:T(8,128)(2,1)}) custom-call(bf16[2,64,16,128]{3,2,1,0:T(8,128)(2,1)} %x_h.1, bf16[2,64,16,128]{3,2,1,0:T(8,128)(2,1)} %s_h.1, bf16[1,64,512]{2,1,0:T(8,128)(2,1)} %c_h.1, bf16[3,3,64,256]{3,2,1,0:T(8,128)(2,1)} %sw_h.1, bf16[3,256,256]{2,1,0:T(8,128)(2,1)} %tw_h.1), custom_call_target="tpu_custom_call" | custom-call | tf_op jit(solution)/shard_map/space_time_backward/pallas_call | solution.py:386
  43.4 1.1 %convert_multiply_fusion = f32[48,16,256]{2,1,0:T(8,128)S(1)} fusion(bf16[48,16,256]{2,1,0:T(8,128)(2,1)} %get-tuple-element.6), kind=kLoop, calls=%fused_computation | loop fusion | flops 393216 | bytes 1179648 | tf_op jit(solution)/shard_map/mul | solution.py:434
  44.5 0.7 %slice.14 = f32[12,16,256]{2,1,0:T(8,128)} slice(f32[48,16,256]{2,1,0:T(8,128)S(1)} %convert_multiply_fusion), slice={[0:12], [0:16], [0:256]} | slice | bytes 393216 | tf_op jit(solution)/shard_map/slice | solution.py:435
  45.2 0.0 copy-start
  45.2 0.9 %slice.13 = f32[36,16,256]{2,1,0:T(8,128)} slice(f32[48,16,256]{2,1,0:T(8,128)S(1)} %convert_multiply_fusion), slice={[12:48], [0:16], [0:256]} | slice | bytes 1179648 | tf_op jit(solution)/shard_map/slice | solution.py:435
  46.1 0.4 copy-done
  46.5 0.8 %copy.9 = bf16[2,64,16,128]{3,2,1,0:T(8,128)(2,1)} copy(bf16[2,64,16,128]{3,2,1,0:T(8,128)(2,1)S(1)} %copy-done) | data formatting | bytes 1048576
Async XLA Ops:
  45.2 1.3 %copy-start = (bf16[2,64,16,128]{3,2,1,0:T(8,128)(2,1)S(1)}, bf16[2,64,16,128]{3,2,1,0:T(8,128)(2,1)}, u32[]{:S(2)}) copy-start(bf16[2,64,16,128]{3,2,1,0:T(8,128)(2,1)} %get-tuple-element.10) | copy-start | bytes 1572868

commit v2 on v1

--- a/solution.py
+++ b/solution.py
@@ -13,6 +13,12 @@
 UNITS = 24
 
 
+FAR_FIRST = sorted(
+    [(i, j, k) for i in range(4) for j in range(4) for k in range(2) if i or j or k],
+    key=lambda s: -(min(s[0], 4 - s[0]) + min(s[1], 4 - s[1]) + s[2]),
+)
+
+
 def dot(a, b):
     return jnp.dot(a, b, preferred_element_type=F32)
 
@@ -23,11 +29,11 @@
 
 def kernel(
     x_h, s_h, c_h, sw_h, tw_h,
-    ig_h, gr_v,
-    x_v, s_v, sw_v, tw_v, ring, halo, pool, q_v, sq_v, a_v, g_v, p_v, xe_v, z_v, out_v,
+    ig_v, gr_v,
+    x_v, s_v, sw_v, tw_v, ring, halo, pool, q_v, sq_v, a_v, g_v, p_v, xe_v, z_v,
     partf, part, xch, half_v, rs_v,
-    load_sem, ring_send, ring_recv, fwd_send, halo_recv,
-    xch_send, xch_recv, rs_send, rs_recv, ag_send, ag_recv, sib_send, sib_recv, out_sem,
+    load_sem, ring_send_sem, ring_recv, fwd_send, halo_recv,
+    xch_send, xch_recv, rs_send, rs_recv, ag_send, ag_recv, sib_send, sib_recv,
 ):
     p = lax.axis_index("frames")
     c = lax.axis_index("chan")
@@ -37,36 +43,37 @@
     column = lax.div(chip, 2)
     z = 2 * c + zl
 
-    def at_z(zz):
-        zz = lax.rem(zz, 8)
+    def in_ring(step):
+        zz = lax.rem(z + step + 8, 8)
         return (4 * column + 2 * lax.rem(zz, 2) + core, lax.div(zz, 2))
 
-    up, down = at_z(z + 1), at_z(z + 7)
+    pair = p + 2 * core - 1
+    paired = jnp.logical_and(pair >= 0, pair < 64)
+
+    def in_pair(step):
+        zz = lax.rem(z + step + 8, 8)
+        return (4 * lax.div(pair, 4) + 2 * lax.rem(zz, 2) + 1 - core, lax.div(zz, 2))
+
     sibling = (p + 1 - 2 * core, c)
-    differ = jnp.where(zl == core, 0, 1)
-    to_step = jnp.where(zl == core, 1 - 2 * core, jnp.where(core == 1, 3, -3))
-    from_step = jnp.where(zl == core, jnp.where(core == 0, -3, 3), jnp.where(core == 1, -1, 1))
-    to_frame, from_frame = p + to_step, p + from_step
-    last = 4 * 16
-    to_ok = jnp.logical_and(to_frame >= 0, to_frame < last)
-    from_ok = jnp.logical_and(from_frame >= 0, from_frame < last)
 
     barrier = pltpu.get_barrier_semaphore()
 
     def greet(device):
         pl.semaphore_signal(barrier, inc=1, device_id=device, device_id_type=pl.DeviceIdType.MESH)
 
-    greet(up)
-    greet(down)
+    greet(in_ring(2))
+    greet(in_ring(-2))
     greet(sibling)
 
-    @pl.when(to_ok)
-    def _():
-        greet((to_frame, c))
-
-    @pl.when(from_ok)
-    def _():
-        greet((from_frame, c))
+    @pl.when(paired)
+    def _():
+        greet(in_pair(1))
+        greet(in_pair(-1))
+
+    x, y = lax.div(chip, 8), lax.rem(column, 4)
+
+    def chip_at(offset):
+        return 8 * lax.rem(x + offset[0], 4) + 2 * lax.rem(y + offset[1], 4) + lax.rem(zl + offset[2], 2)
 
     def greet_chip(j, carry):
         greet((2 * lax.rem(chip + j, CHIPS) + core, c))
@@ -75,7 +82,7 @@
     lax.fori_loop(1, CHIPS, greet_chip, 0)
 
     loads = [
-        pltpu.make_async_copy(c_h.at[0], ring.at[0, c], load_sem.at[0]),
+        pltpu.make_async_copy(c_h.at[0], ring.at[c], load_sem.at[0]),
         pltpu.make_async_copy(s_h, s_v, load_sem.at[1]),
         pltpu.make_async_copy(x_h, x_v, load_sem.at[2]),
         pltpu.make_async_copy(tw_h, tw_v, load_sem.at[3]),
@@ -84,9 +91,7 @@
     for load in loads:
         load.start()
 
-    pl.semaphore_wait(
-        barrier, 34 + jnp.where(to_ok, 1, 0) + jnp.where(from_ok, 1, 0)
-    )
+    pl.semaphore_wait(barrier, 34 + jnp.where(paired, 2, 0))
 
     def remote(src, dst, send, recv, device):
         return pltpu.make_async_remote_copy(
@@ -99,52 +104,61 @@
     def rows(half):
         return pl.ds(32 * half, 32)
 
-    def ring_send_step(way, step, half):
-        zz = z + (8 - step if way == 0 else step)
-        quarter = lax.div(lax.rem(zz, 8), 2)
-        if step == 0:
-            src = c_h.at[0, rows(half)]
-        else:
-            src = ring.at[step % 2, quarter, rows(half)]
+    quarters = {step: lax.rem(c + step + 4, 4) for step in (-1, 0, 1, 2)}
+
+    def ring_send(hop, quarter, half, index, src=None):
         copy = remote(
-            src, ring.at[(step + 1) % 2, quarter, rows(half)],
-            ring_send.at[way, step, half], ring_recv.at[way, step, half],
-            up if way == 0 else down,
+            ring.at[quarter, rows(half)] if src is None else src, ring.at[quarter, rows(half)],
+            ring_send_sem.at[index], ring_recv.at[index], in_ring(hop),
         )
         copy.start()
         sent.append(copy)
 
-    def ring_wait_step(way, step, half):
-        zz = z + (7 - step if way == 0 else 1 + step)
-        quarter = lax.div(lax.rem(zz, 8), 2)
-        dst = ring.at[(step + 1) % 2, quarter, rows(half)]
-        remote(
-            dst, dst, ring_send.at[way, step, half], ring_recv.at[way, step, half],
-            down if way == 0 else up,
-        ).wait_recv()
-        return quarter
-
-    def forward_own(src, quarter, index):
+    def ring_wait(quarter, half, index):
+        dst = ring.at[quarter, rows(half)]
+        remote(dst, dst, ring_send_sem.at[index], ring_recv.at[index], sibling).wait_recv()
+
+    def to_sibling(src, quarter, index):
         copy = remote(src, halo.at[core, quarter], fwd_send.at[index], halo_recv.at[0], sibling)
         copy.start()
         sent.append(copy)
 
-    def forward_other(quarter, index):
+    pair_copies = []
+
+    def to_pair(step, src, quarter, index):
         copy = remote(
-            ring.at[1, quarter], halo.at[1 - core, quarter],
-            fwd_send.at[index], halo_recv.at[1], (to_frame, c),
+            src, halo.at[1 - core, quarter], fwd_send.at[index], halo_recv.at[1], in_pair(step)
         )
 
-        @pl.when(to_ok)
+        @pl.when(paired)
         def _():
             copy.start()
 
-        return copy
+        pair_copies.append(copy)
 
     for half in range(2):
-        ring_send_step(0, 0, half)
-        ring_send_step(1, 0, half)
-    forward_own(c_h.at[0], c, 0)
+        ring_send(2, c, half, half, c_h.at[0, rows(half)])
+        ring_send(-2, c, half, 2 + half, c_h.at[0, rows(half)])
+    to_pair(1, c_h.at[0], c, 4)
+    to_pair(-1, c_h.at[0], c, 5)
+    to_sibling(c_h.at[0], c, 0)
+
+    def near_shards():
+        ring_wait(quarters[-1], 0, 0)
+        ring_send(2, quarters[-1], 0, 4)
+        ring_wait(quarters[1], 0, 2)
+        ring_wait(quarters[1], 1, 3)
+        ring_send(-2, quarters[1], 1, 5)
+        ring_wait(quarters[-1], 1, 1)
+        to_pair(1, ring.at[quarters[-1]], quarters[-1], 6)
+        to_pair(-1, ring.at[quarters[1]], quarters[1], 7)
+        to_sibling(ring.at[quarters[-1]], quarters[-1], 1)
+        to_sibling(ring.at[quarters[1]], quarters[1], 2)
+
+    def far_shard():
+        ring_wait(quarters[2], 0, 4)
+        ring_wait(quarters[2], 1, 5)
+        to_sibling(ring.at[quarters[2]], quarters[2], 3)
 
     lane = lax.broadcasted_iota(jnp.int32, (128, 384), 1)
     column_of = lax.broadcasted_iota(jnp.int32, (128, 384), 0)
@@ -165,30 +179,12 @@
             lower = height[4 * j + 2] + height[4 * j + 3]
             sq_v[pl.ds(64 * f, 64), 128 * j : 128 * j + 128] = jnp.where(low, upper, lower).astype(BF)
 
-    others = []
-
-    def ring_step(step):
-        for way in range(2):
-            for half in range(2):
-                if step == 3 and half != way:
-                    continue
-                quarter = ring_wait_step(way, step, half)
-                if step < 2 or (step == 2 and half == way):
-                    ring_send_step(way, step + 1, half)
-            if step == 0 or step == 2:
-                others.append(forward_other(quarter, 4 + step + way))
-            elif step == 1:
-                forward_own(ring.at[0, quarter], quarter, 1 + way)
-        if step == 3:
-            forward_own(ring.at[0, quarter], quarter, 3)
-
-    ring_step(0)
     loads[2].wait()
     for f in range(2):
         sums = dot(x_v[f].reshape(1024, 128), pairs)
         for b in range(3):
             pool[1 + b, pl.ds(f * 1024, 1024), :] = sums[:, 128 * b : 128 * b + 128]
-    ring_step(1)
+    near_shards()
     for f in range(2):
         for b in range(3):
             height = [pool[1 + b, pl.ds(f * 1024 + h, 64, stride=16), :] for h in range(16)]
@@ -200,25 +196,23 @@
                     q_v[f, pl.ds((3 * a + b) * 64, 64), 128 * j : 128 * j + 128] = jnp.where(
                         low, total[4 * j + a], total[4 * j + a + 2]
                     ).astype(BF)
-        if f == 0:
-            ring_step(2)
     loads[0].wait()
     loads[3].wait()
-    ring_step(3)
-
-    own = ring[0].reshape(256, 512)
+    far_shard()
+
+    own = ring[...].reshape(256, 512)
     a_v[...] = dot(tw_v[...].reshape(768, 256), own)
     t_own = dot_nt(sq_v[...], own)
 
     dst = halo.at[1 - core]
     pltpu.make_async_copy(dst, dst, halo_recv.at[0]).wait()
 
-    @pl.when(from_ok)
+    @pl.when(paired)
     def _():
         dst = halo.at[core]
         pltpu.make_async_copy(dst, dst, halo_recv.at[1]).wait()
 
-    @pl.when(jnp.logical_not(from_ok))
+    @pl.when(jnp.logical_not(paired))
     def _():
         halo[core] = jnp.zeros((4, 64, 512), BF)
 
@@ -282,10 +276,7 @@
                 for k in range(2):
                     h = 2 * (2 * j + k) + r
                     z_v[pl.ds(h, 64, stride=16), :] = woven[r, j, :, 128 * k : 128 * k + 128]
-        out_v[f] = z_v[...].reshape(64, 16, 128).astype(BF)
-        copy = pltpu.make_async_copy(out_v.at[f], ig_h.at[f], out_sem.at[f])
-        copy.start()
-        return copy
+        ig_v[f] = z_v[...].reshape(64, 16, 128).astype(BF)
 
     loads[4].wait()
     input_products(0)
@@ -293,30 +284,23 @@
     exchange.wait_recv()
     half_v[...] = (partf[mine] + xch[...].astype(F32)).astype(BF)
 
-    def owner_loop(body):
-        def group(g, carry):
-            for r in range(3):
-                body(3 * g + r, 4 * g + r + core)
-            return carry
-
-        lax.fori_loop(0, 8, group, 0)
-
-    def scatter(unit, owner):
-        @pl.when(owner != chip)
+    for slot, offset in enumerate(FAR_FIRST):
+        owner = chip_at(offset)
+        owner_place = lax.rem(owner, 4) - core
+
+        @pl.when(jnp.logical_and(owner_place >= 0, owner_place < 3))
         def _():
-            slot = lax.rem(chip - owner + 63, CHIPS)
+            unit = 3 * lax.div(owner, 4) + owner_place
             remote(
                 half_v.at[unit], rs_v.at[slot], rs_send, rs_recv, (2 * owner + core, c)
             ).start()
 
-    owner_loop(scatter)
-
     place_in_group = lax.rem(chip, 4) - core
     is_owner = jnp.logical_and(place_in_group >= 0, place_in_group < 3)
     my_unit = 3 * lax.div(chip, 4) + place_in_group
 
     input_parities(0)
-    out_copies = [input_output(0)]
+    input_output(0)
 
     @pl.when(is_owner)
     def _():
@@ -327,17 +311,13 @@
             total = total + rs_v[slot].astype(F32)
         gr_v[core * UNITS + my_unit] = total.astype(BF)
 
-        def spread(j, carry):
+        for offset in FAR_FIRST:
             src = gr_v.at[core * UNITS + my_unit]
-            device = (2 * lax.rem(chip + j, CHIPS) + core, c)
-            remote(src, src, ag_send, ag_recv, device).start()
-            return carry
-
-        lax.fori_loop(1, CHIPS, spread, 0)
+            remote(src, src, ag_send, ag_recv, (2 * chip_at(offset) + core, c)).start()
 
     input_products(1)
     input_parities(1)
-    out_copies.append(input_output(1))
+    input_output(1)
 
     @pl.when(is_owner)
     def _():
@@ -355,9 +335,9 @@
     for copy in sent:
         copy.wait_send()
 
-    @pl.when(to_ok)
-    def _():
-        for copy in others:
+    @pl.when(paired)
+    def _():
+        for copy in pair_copies:
             copy.wait_send()
 
     exchange.wait_send()
@@ -374,24 +354,35 @@
         src = half_v.at[pl.ds(0, UNITS)]
         pltpu.make_async_copy(src, src, rs_send).wait()
 
-    for copy in out_copies:
-        copy.wait()
     handover.wait()
 
 
+def finish(ig_v, gr_v, ig_out, sp_out, te_out, wide_v, sem):
+    scale = 1.0 / math.sqrt(128 * 16 * 128)
+    stores = [pltpu.make_async_copy(ig_v, ig_out, sem.at[4])]
+    stores[0].start()
+    for k in range(4):
+        wide_v[12 * k : 12 * k + 12] = gr_v[12 * k : 12 * k + 12].astype(F32) * scale
+        dst = te_out if k == 0 else sp_out.at[pl.ds(12 * k - 12, 12)]
+        store = pltpu.make_async_copy(wide_v.at[pl.ds(12 * k, 12)], dst, sem.at[k])
+        store.start()
+        stores.append(store)
+    for store in stores:
+        store.wait()
+
+
 def shards(inputs, saved, cotangent, spatial_w, temporal_w):
-    scale = 1.0 / math.sqrt(128 * 16 * 128)
     vmem = pltpu.VMEM
     dma = pltpu.SemaphoreType.DMA
     input_grad, grads = pl.pallas_call(
         kernel,
         out_shape=(
-            jax.ShapeDtypeStruct((2, 64, 16, 128), BF),
-            jax.ShapeDtypeStruct((2 * UNITS, 16, 256), BF),
+            pltpu.VMEM((2, 64, 16, 128), BF),
+            pltpu.VMEM((2 * UNITS, 16, 256), BF),
         ),
         in_specs=[pl.BlockSpec(memory_space=pl.ANY)] * 5,
         out_specs=(
-            pl.BlockSpec(memory_space=pl.ANY),
+            pl.BlockSpec(memory_space=pltpu.VMEM),
             pl.BlockSpec(memory_space=pltpu.VMEM),
         ),
         scratch_shapes=[
@@ -399,7 +390,7 @@
             vmem((2, 64, 16, 128), BF),
             vmem((3, 3, 64, 256), BF),
             vmem((3, 256, 256), BF),
-            vmem((2, 4, 64, 512), BF),
+            vmem((4, 64, 512), BF),
             vmem((2, 4, 64, 512), BF),
             vmem((4, 2048, 128), F32),
             vmem((2, 576, 512), BF),
@@ -409,30 +400,44 @@
             vmem((9, 64, 512), F32),
             vmem((2, 4, 64, 256), BF),
             vmem((1024, 128), F32),
-            vmem((2, 64, 16, 128), BF),
             vmem((2 * UNITS, 16, 256), F32),
             vmem((2 * UNITS, 16, 256), BF),
             vmem((UNITS, 16, 256), BF),
             vmem((UNITS, 16, 256), BF),
             vmem((CHIPS - 1, 16, 256), BF),
             dma((5,)),
-            dma((2, 4, 2)),
-            dma((2, 4, 2)),
+            dma((6,)),
+            dma((6,)),
             dma((8,)),
             dma((2,)),
             dma, dma,
             dma, dma,
             dma, dma,
             dma, dma,
-            dma((2,)),
         ],
         compiler_params=pltpu.CompilerParams(
             collective_id=0, has_side_effects=True, vmem_limit_bytes=56 * 1024 * 1024
         ),
         name="space_time_backward",
     )(inputs, saved, cotangent, spatial_w, temporal_w)
-    grads = grads.reshape(12, 64, 256).astype(F32) * scale
-    return (input_grad, grads[3:].reshape(3, 3, 64, 256), grads[:3])
+    input_grad = pltpu.with_memory_space_constraint(input_grad, pltpu.VMEM)
+    grads = pltpu.with_memory_space_constraint(grads, pltpu.VMEM)
+    input_grad, spatial, temporal = pl.pallas_call(
+        finish,
+        out_shape=(
+            jax.ShapeDtypeStruct((2, 64, 16, 128), BF),
+            jax.ShapeDtypeStruct((36, 16, 256), F32),
+            jax.ShapeDtypeStruct((12, 16, 256), F32),
+        ),
+        in_specs=[pl.BlockSpec(memory_space=pltpu.VMEM)] * 2,
+        out_specs=[pl.BlockSpec(memory_space=pl.ANY)] * 3,
+        scratch_shapes=[
+            vmem((2 * UNITS, 16, 256), F32),
+            dma((5,)),
+        ],
+        name="scale_gradients",
+    )(input_grad, grads)
+    return (input_grad, spatial.reshape(3, 3, 64, 256), temporal.reshape(3, 64, 256))
 
 
 def solution(mesh):

time: 47.4 us -> 38.8 us (0.82)
  Pallas kernels: 42.8 us -> 38.1 us
  local copies, waits for them, and re-layouts: 2.74 us -> 0 us
  other arithmetic: 1.08 us -> 0 us
    pallas_call x1 -> x2, Pallas kernels: 42.8 us -> 38.1 us  [the longest x1 37 us: shards(): pl.pallas_call(kernel, out_shape=(pltpu.VMEM((2, 64, 16, 128), BF), pltpu...]
    slice x2 -> x0, local copies, waits for them, and re-layouts: 1.55 us -> none  [shards(): return (input_grad, grads[3:].reshape(3, 3, 64, 256), grads[:3])]
    unnamed x3 -> x0, local copies, waits for them, and re-layouts: 1.19 us -> none
    mul x1 -> x0, other arithmetic: 1.08 us -> none  [shards(): grads = grads.reshape(12, 64, 256).astype(F32) * scale]
where the time goes in v2:
time: 38.8 us; the launch traced here: 38.7 us
  Pallas kernels  38.1 us (98%)
  between operations  0.64 us (2%)
    pallas_call x1, Pallas kernels, shards(): pl.pallas_call(kernel, out_shape=(pltpu.VMEM((2, 64, 16, 128), BF), pltpu...  37 us
    pallas_call x1, Pallas kernels, shards(): pl.pallas_call(finish, out_shape=(jax.ShapeDtypeStruct((2, 64, 16, 128),...  1.09 us

profile of v2, /device:TPU:1, one launch (start us, length us, event | category | flops | bytes accessed | tf_op | source)
XLA Modules:
  0.0 38.7 jit_solution(4073293522519146367)
XLA Ops:
  0.6 37.0 %space_time_backward.1 = (bf16[2,64,16,128]{3,2,1,0:T(8,128)(2,1)S(1)}, bf16[48,16,256]{2,1,0:T(8,128)(2,1)S(1)}) custom-call(bf16[2,64,16,128]{3,2,1,0:T(8,128)(2,1)} %x_h.1, bf16[2,64,16,128]{3,2,1,0:T(8,128)(2,1)} %s_h.1, bf16[1,64,512]{2,1,0:T(8,128)(2,1)} %c_h.1, bf16[3,3,64,256]{3,2,1,0:T(8,128)(2,1)} %sw_h.1, bf16[3,256,256]{2,1,0:T(8,128)(2,1)} %tw_h.1), custom_call_target="tpu_custom_call" | custom-call | tf_op jit(solution)/shard_map/space_time_backward/pallas_call | solution.py:377
  37.6 1.1 %scale_gradients.1 = (bf16[2,64,16,128]{3,2,1,0:T(8,128)(2,1)}, f32[36,16,256]{2,1,0:T(8,128)}, f32[12,16,256]{2,1,0:T(8,128)}) custom-call(bf16[2,64,16,128]{3,2,1,0:T(8,128)(2,1)S(1)} %get-tuple-element.8.ig_v, bf16[48,16,256]{2,1,0:T(8,128)(2,1)S(1)} %get-tuple-element.9.gr_v), custom_call_target="tpu_custom_call" | custom-call | tf_op jit(solution)/shard_map/scale_gradients/pallas_call | solution.py:425

commit v3 on v2

--- a/solution.py
+++ b/solution.py
@@ -10,7 +10,7 @@
 BF = jnp.bfloat16
 F32 = jnp.float32
 CHIPS = 32
-UNITS = 24
+PIECES = 48
 
 
 FAR_FIRST = sorted(
@@ -19,6 +19,10 @@
 )
 
 
+NEXT = [(1, 0, 0), (3, 0, 0), (0, 1, 0), (0, 3, 0), (0, 0, 1)]
+ROUNDS = 4
+
+
 def dot(a, b):
     return jnp.dot(a, b, preferred_element_type=F32)
 
@@ -31,9 +35,9 @@
     x_h, s_h, c_h, sw_h, tw_h,
     ig_v, gr_v,
     x_v, s_v, sw_v, tw_v, ring, halo, pool, q_v, sq_v, a_v, g_v, p_v, xe_v, z_v,
-    partf, part, xch, half_v, rs_v,
+    given, kept, xch, half_v, rs_v,
     load_sem, ring_send_sem, ring_recv, fwd_send, halo_recv,
-    xch_send, xch_recv, rs_send, rs_recv, ag_send, ag_recv, sib_send, sib_recv,
+    xch_send, xch_recv, rs_send, rs_recv, ag_send, ag_recv, sib_send, sib_recv, news,
 ):
     p = lax.axis_index("frames")
     c = lax.axis_index("chan")
@@ -75,11 +79,8 @@
     def chip_at(offset):
         return 8 * lax.rem(x + offset[0], 4) + 2 * lax.rem(y + offset[1], 4) + lax.rem(zl + offset[2], 2)
 
-    def greet_chip(j, carry):
-        greet((2 * lax.rem(chip + j, CHIPS) + core, c))
-        return carry
-
-    lax.fori_loop(1, CHIPS, greet_chip, 0)
+    for offset in NEXT:
+        greet((2 * chip_at(offset) + core, c))
 
     loads = [
         pltpu.make_async_copy(c_h.at[0], ring.at[c], load_sem.at[0]),
@@ -91,7 +92,8 @@
     for load in loads:
         load.start()
 
-    pl.semaphore_wait(barrier, 34 + jnp.where(paired, 2, 0))
+    pl.semaphore_wait(barrier, 3 + len(NEXT) + jnp.where(paired, 2, 0))
+    loads[0].wait()
 
     def remote(src, dst, send, recv, device):
         return pltpu.make_async_remote_copy(
@@ -137,11 +139,11 @@
         pair_copies.append(copy)
 
     for half in range(2):
-        ring_send(2, c, half, half, c_h.at[0, rows(half)])
-        ring_send(-2, c, half, 2 + half, c_h.at[0, rows(half)])
-    to_pair(1, c_h.at[0], c, 4)
-    to_pair(-1, c_h.at[0], c, 5)
-    to_sibling(c_h.at[0], c, 0)
+        ring_send(2, c, half, half, ring.at[c, rows(half)])
+        ring_send(-2, c, half, 2 + half, ring.at[c, rows(half)])
+    to_pair(1, ring.at[c], c, 4)
+    to_pair(-1, ring.at[c], c, 5)
+    to_sibling(ring.at[c], c, 0)
 
     def near_shards():
         ring_wait(quarters[-1], 0, 0)
@@ -160,6 +162,18 @@
         ring_wait(quarters[2], 1, 5)
         to_sibling(ring.at[quarters[2]], quarters[2], 3)
 
+    def spread_news(k):
+        for offset in NEXT:
+            pl.semaphore_signal(
+                news.at[k], inc=1, device_id=(2 * chip_at(offset) + core, c),
+                device_id_type=pl.DeviceIdType.MESH,
+            )
+
+    def hear_news(k):
+        pl.semaphore_wait(news.at[k], len(NEXT))
+
+    spread_news(0)
+
     lane = lax.broadcasted_iota(jnp.int32, (128, 384), 1)
     column_of = lax.broadcasted_iota(jnp.int32, (128, 384), 0)
     first = 2 * (lane & 63) + (lane >> 7) - 1
@@ -179,11 +193,15 @@
             lower = height[4 * j + 2] + height[4 * j + 3]
             sq_v[pl.ds(64 * f, 64), 128 * j : 128 * j + 128] = jnp.where(low, upper, lower).astype(BF)
 
+    hear_news(0)
+    spread_news(1)
     loads[2].wait()
     for f in range(2):
         sums = dot(x_v[f].reshape(1024, 128), pairs)
         for b in range(3):
             pool[1 + b, pl.ds(f * 1024, 1024), :] = sums[:, 128 * b : 128 * b + 128]
+    hear_news(1)
+    spread_news(2)
     near_shards()
     for f in range(2):
         for b in range(3):
@@ -196,8 +214,9 @@
                     q_v[f, pl.ds((3 * a + b) * 64, 64), 128 * j : 128 * j + 128] = jnp.where(
                         low, total[4 * j + a], total[4 * j + a + 2]
                     ).astype(BF)
-    loads[0].wait()
     loads[3].wait()
+    hear_news(2)
+    spread_news(3)
     far_shard()
 
     own = ring[...].reshape(256, 512)
@@ -222,23 +241,40 @@
     g_v[0] = ((a_v[0:256] + middle + dot(tw_v[2], before)) * 0.125).astype(BF)
     g_v[1] = ((dot(tw_v[0], after) + middle + a_v[512:768]) * 0.125).astype(BF)
 
-    t_after = dot_nt(sq_v[64:128], after)
-    t_before = dot_nt(sq_v[0:64], before)
-    temporal = [
-        (t_own[0:64] + t_after) * 0.125,
-        (t_own[0:64] + t_own[64:128]) * 0.125,
-        (t_own[64:128] + t_before) * 0.125,
-    ]
-    for k in range(3):
-        partf[4 * k : 4 * k + 4] = temporal[k].reshape(4, 16, 256)
-    spatial = dot_nt(q_v[0], g_v[0]) + dot_nt(q_v[1], g_v[1])
-    partf[12:48] = spatial.reshape(36, 16, 256)
-    part[...] = partf[...].astype(BF)
-
-    mine = pl.ds(core * UNITS, UNITS)
-    theirs = pl.ds((1 - core) * UNITS, UNITS)
-    exchange = remote(part.at[theirs], xch, xch_send, xch_recv, sibling)
-    exchange.start()
+    def put(dst, at, value):
+        count = value.shape[0] // 16
+        for side in range(2):
+            piece = value[:, 128 * side : 128 * side + 128].reshape(count, 16, 128)
+            dst[at : at + count, side] = piece.astype(dst.dtype)
+
+    def spatial(dst, at, first_tap, last_tap):
+        taps = slice(64 * first_tap, 64 * last_tap)
+        put(dst, at, dot_nt(q_v[0, taps], g_v[0]) + dot_nt(q_v[1, taps], g_v[1]))
+
+    def lower_half(dst):
+        t_after = dot_nt(sq_v[64:128], after)
+        t_before = dot_nt(sq_v[0:64], before)
+        put(dst, 0, (t_own[0:64] + t_after) * 0.125)
+        put(dst, 4, (t_own[0:64] + t_own[64:128]) * 0.125)
+        put(dst, 8, (t_own[64:128] + t_before) * 0.125)
+        spatial(dst, 12, 0, 3)
+
+    def upper_half(dst):
+        spatial(dst, 0, 3, 9)
+
+    exchange = remote(given, xch, xch_send, xch_recv, sibling)
+
+    @pl.when(core == 0)
+    def _():
+        upper_half(given)
+        exchange.start()
+        lower_half(kept)
+
+    @pl.when(core == 1)
+    def _():
+        lower_half(given)
+        exchange.start()
+        upper_half(kept)
 
     def input_products(f):
         p_v[...] = dot(sw_v[...].reshape(576, 256), g_v[f]).reshape(9, 64, 512)
@@ -278,57 +314,74 @@
                     z_v[pl.ds(h, 64, stride=16), :] = woven[r, j, :, 128 * k : 128 * k + 128]
         ig_v[f] = z_v[...].reshape(64, 16, 128).astype(BF)
 
+    exchange.wait_recv()
+    half_v[...] = (kept[...] + xch[...].astype(F32)).astype(BF).reshape(PIECES, 16, 128)
+    hear_news(3)
+
+    large = lax.rem(x + y + zl + core, 2) == 0
+    large_at, small_at = 2 * column, 32 + column
+
+    for slot, offset in enumerate(FAR_FIRST):
+        owner = chip_at(offset)
+        owner_column = lax.div(owner, 2)
+        owner_large = large if sum(offset) % 2 == 0 else jnp.logical_not(large)
+
+        @pl.when(owner_large)
+        def _():
+            remote(
+                half_v.at[pl.ds(2 * owner_column, 2)], rs_v.at[pl.ds(2 * slot, 2)],
+                rs_send, rs_recv, (2 * owner + core, c),
+            ).start()
+
+        @pl.when(jnp.logical_not(owner_large))
+        def _():
+            remote(
+                half_v.at[pl.ds(32 + owner_column, 1)], rs_v.at[pl.ds(slot, 1)],
+                rs_send, rs_recv, (2 * owner + core, c),
+            ).start()
+
     loads[4].wait()
     input_products(0)
-
-    exchange.wait_recv()
-    half_v[...] = (partf[mine] + xch[...].astype(F32)).astype(BF)
-
-    for slot, offset in enumerate(FAR_FIRST):
-        owner = chip_at(offset)
-        owner_place = lax.rem(owner, 4) - core
-
-        @pl.when(jnp.logical_and(owner_place >= 0, owner_place < 3))
-        def _():
-            unit = 3 * lax.div(owner, 4) + owner_place
-            remote(
-                half_v.at[unit], rs_v.at[slot], rs_send, rs_recv, (2 * owner + core, c)
-            ).start()
-
-    place_in_group = lax.rem(chip, 4) - core
-    is_owner = jnp.logical_and(place_in_group >= 0, place_in_group < 3)
-    my_unit = 3 * lax.div(chip, 4) + place_in_group
-
     input_parities(0)
     input_output(0)
 
-    @pl.when(is_owner)
-    def _():
-        dst = rs_v.at[pl.ds(0, CHIPS - 1)]
+    def own_piece(at, count):
+        dst = rs_v.at[pl.ds(0, count * (CHIPS - 1))]
         pltpu.make_async_copy(dst, dst, rs_recv).wait()
-        total = half_v[my_unit].astype(F32)
+        total = half_v[pl.ds(at, count)].astype(F32)
         for slot in range(CHIPS - 1):
-            total = total + rs_v[slot].astype(F32)
-        gr_v[core * UNITS + my_unit] = total.astype(BF)
-
+            total = total + rs_v[count * slot : count * slot + count].astype(F32)
+        here = pl.ds(core * PIECES + at, count)
+        gr_v[here] = total.astype(BF)
         for offset in FAR_FIRST:
-            src = gr_v.at[core * UNITS + my_unit]
+            src = gr_v.at[here]
             remote(src, src, ag_send, ag_recv, (2 * chip_at(offset) + core, c)).start()
+
+    @pl.when(large)
+    def _():
+        own_piece(large_at, 2)
+
+    @pl.when(jnp.logical_not(large))
+    def _():
+        own_piece(small_at, 1)
 
     input_products(1)
     input_parities(1)
     input_output(1)
 
-    @pl.when(is_owner)
-    def _():
-        dst = gr_v.at[pl.ds(0, UNITS - 1)]
-        pltpu.make_async_copy(dst, dst, ag_recv).wait()
-
-    @pl.when(jnp.logical_not(is_owner))
-    def _():
-        dst = gr_v.at[pl.ds(0, UNITS)]
-        pltpu.make_async_copy(dst, dst, ag_recv).wait()
-
+    def rest(count, sem):
+        dst = gr_v.at[pl.ds(0, count)]
+        pltpu.make_async_copy(dst, dst, sem).wait()
+
+    @pl.when(large)
+    def _():
+        rest(PIECES - 2, ag_recv)
+
+    @pl.when(jnp.logical_not(large))
+    def _():
+        rest(PIECES - 1, ag_recv)
+
+    mine = pl.ds(core * PIECES, PIECES)
     handover = remote(gr_v.at[mine], gr_v.at[mine], sib_send, sib_recv, sibling)
     handover.start()
 
@@ -342,17 +395,15 @@
 
     exchange.wait_send()
 
-    @pl.when(is_owner)
-    def _():
-        src = half_v.at[pl.ds(0, UNITS - 1)]
-        pltpu.make_async_copy(src, src, rs_send).wait()
-        src = rs_v.at[pl.ds(0, CHIPS - 1)]
-        pltpu.make_async_copy(src, src, ag_send).wait()
-
-    @pl.when(jnp.logical_not(is_owner))
-    def _():
-        src = half_v.at[pl.ds(0, UNITS)]
-        pltpu.make_async_copy(src, src, rs_send).wait()
+    @pl.when(large)
+    def _():
+        rest(PIECES - 2, rs_send)
+        rest(2 * (CHIPS - 1), ag_send)
+
+    @pl.when(jnp.logical_not(large))
+    def _():
+        rest(PIECES - 1, rs_send)
+        rest(CHIPS - 1, ag_send)
 
     handover.wait()
 
@@ -362,7 +413,11 @@
     stores = [pltpu.make_async_copy(ig_v, ig_out, sem.at[4])]
     stores[0].start()
     for k in range(4):
-        wide_v[12 * k : 12 * k + 12] = gr_v[12 * k : 12 * k + 12].astype(F32) * scale
+        pieces = gr_v[24 * k : 24 * k + 24].reshape(12, 2, 16, 128)
+        for side in range(2):
+            wide_v[12 * k : 12 * k + 12, :, 128 * side : 128 * side + 128] = (
+                pieces[:, side].astype(F32) * scale
+            )
         dst = te_out if k == 0 else sp_out.at[pl.ds(12 * k - 12, 12)]
         store = pltpu.make_async_copy(wide_v.at[pl.ds(12 * k, 12)], dst, sem.at[k])
         store.start()
@@ -378,7 +433,7 @@
         kernel,
         out_shape=(
             pltpu.VMEM((2, 64, 16, 128), BF),
-            pltpu.VMEM((2 * UNITS, 16, 256), BF),
+            pltpu.VMEM((2 * PIECES, 16, 128), BF),
         ),
         in_specs=[pl.BlockSpec(memory_space=pl.ANY)] * 5,
         out_specs=(
@@ -400,11 +455,11 @@
             vmem((9, 64, 512), F32),
             vmem((2, 4, 64, 256), BF),
             vmem((1024, 128), F32),
-            vmem((2 * UNITS, 16, 256), F32),
-            vmem((2 * UNITS, 16, 256), BF),
-            vmem((UNITS, 16, 256), BF),
-            vmem((UNITS, 16, 256), BF),
-            vmem((CHIPS - 1, 16, 256), BF),
+            vmem((24, 2, 16, 128), BF),
+            vmem((24, 2, 16, 128), F32),
+            vmem((24, 2, 16, 128), BF),
+            vmem((PIECES, 16, 128), BF),
+            vmem((2 * (CHIPS - 1), 16, 128), BF),
             dma((5,)),
             dma((6,)),
             dma((6,)),
@@ -414,6 +469,7 @@
             dma, dma,
             dma, dma,
             dma, dma,
+            pltpu.SemaphoreType.REGULAR((ROUNDS,)),
         ],
         compiler_params=pltpu.CompilerParams(
             collective_id=0, has_side_effects=True, vmem_limit_bytes=56 * 1024 * 1024
@@ -432,7 +488,7 @@
         in_specs=[pl.BlockSpec(memory_space=pltpu.VMEM)] * 2,
         out_specs=[pl.BlockSpec(memory_space=pl.ANY)] * 3,
         scratch_shapes=[
-            vmem((2 * UNITS, 16, 256), F32),
+            vmem((48, 16, 256), F32),
             dma((5,)),
         ],
         name="scale_gradients",

time: 38.8 us -> 36.5 us (0.941)
  Pallas kernels: 38.1 us -> 35.7 us
    pallas_call x1, Pallas kernels: 37 us -> 34.7 us  [shards(): pl.pallas_call(kernel, out_shape=(pltpu.VMEM((2, 64, 16, 128), BF), pltpu...]
where the time goes in v3:
time: 36.5 us; the launch traced here: 36.4 us
  Pallas kernels  35.7 us (98%)
  between operations  0.64 us (2%)
    pallas_call x1, Pallas kernels, shards(): pl.pallas_call(kernel, out_shape=(pltpu.VMEM((2, 64, 16, 128), BF), pltpu...  34.7 us
    pallas_call x1, Pallas kernels, shards(): pl.pallas_call(finish, out_shape=(jax.ShapeDtypeStruct((2, 64, 16, 128),...  1.09 us

profile of v3, /device:TPU:1, one launch (start us, length us, event | category | flops | bytes accessed | tf_op | source)
XLA Modules:
  0.0 36.4 jit_solution(10801073906089684486)
XLA Ops:
  0.6 34.7 %space_time_backward.1 = (bf16[2,64,16,128]{3,2,1,0:T(8,128)(2,1)S(1)}, bf16[96,16,128]{2,1,0:T(8,128)(2,1)S(1)}) custom-call(bf16[2,64,16,128]{3,2,1,0:T(8,128)(2,1)} %x_h.1, bf16[2,64,16,128]{3,2,1,0:T(8,128)(2,1)} %s_h.1, bf16[1,64,512]{2,1,0:T(8,128)(2,1)} %c_h.1, bf16[3,3,64,256]{3,2,1,0:T(8,128)(2,1)} %sw_h.1, bf16[3,256,256]{2,1,0:T(8,128)(2,1)} %tw_h.1), custom_call_target="tpu_custom_call" | custom-call | tf_op jit(solution)/shard_map/space_time_backward/pallas_call | solution.py:432
  35.3 1.1 %scale_gradients.1 = (bf16[2,64,16,128]{3,2,1,0:T(8,128)(2,1)}, f32[36,16,256]{2,1,0:T(8,128)}, f32[12,16,256]{2,1,0:T(8,128)}) custom-call(bf16[2,64,16,128]{3,2,1,0:T(8,128)(2,1)S(1)} %get-tuple-element.8.ig_v, bf16[96,16,128]{2,1,0:T(8,128)(2,1)S(1)} %get-tuple-element.9.gr_v), custom_call_target="tpu_custom_call" | custom-call | tf_op jit(solution)/shard_map/scale_gradients/pallas_call | solution.py:481

commit v4 on v3

--- a/solution.py
+++ b/solution.py
@@ -127,9 +127,10 @@
 
     pair_copies = []
 
-    def to_pair(step, src, quarter, index):
+    def to_pair(step, src, quarter, index, dst=None):
         copy = remote(
-            src, halo.at[1 - core, quarter], fwd_send.at[index], halo_recv.at[1], in_pair(step)
+            src, halo.at[1 - core, quarter] if dst is None else dst,
+            fwd_send.at[index], halo_recv.at[1], in_pair(step),
         )
 
         @pl.when(paired)
@@ -138,24 +139,33 @@
 
         pair_copies.append(copy)
 
+    def to_pair_half(step, quarter, half, index):
+        to_pair(
+            step, ring.at[quarter, rows(half)], quarter, index,
+            halo.at[1 - core, quarter, rows(half)],
+        )
+
     for half in range(2):
         ring_send(2, c, half, half, ring.at[c, rows(half)])
-        ring_send(-2, c, half, 2 + half, ring.at[c, rows(half)])
+        ring_send(-2, c, 1 - half, 3 - half, ring.at[c, rows(1 - half)])
     to_pair(1, ring.at[c], c, 4)
     to_pair(-1, ring.at[c], c, 5)
     to_sibling(ring.at[c], c, 0)
 
     def near_shards():
-        ring_wait(quarters[-1], 0, 0)
-        ring_send(2, quarters[-1], 0, 4)
-        ring_wait(quarters[1], 0, 2)
-        ring_wait(quarters[1], 1, 3)
-        ring_send(-2, quarters[1], 1, 5)
-        ring_wait(quarters[-1], 1, 1)
-        to_pair(1, ring.at[quarters[-1]], quarters[-1], 6)
-        to_pair(-1, ring.at[quarters[1]], quarters[1], 7)
-        to_sibling(ring.at[quarters[-1]], quarters[-1], 1)
-        to_sibling(ring.at[quarters[1]], quarters[1], 2)
+        below, above = quarters[-1], quarters[1]
+        ring_wait(below, 0, 0)
+        ring_send(2, below, 0, 4)
+        ring_wait(above, 1, 3)
+        ring_send(-2, above, 1, 5)
+        to_pair_half(1, below, 0, 6)
+        to_pair_half(-1, above, 1, 8)
+        ring_wait(below, 1, 1)
+        to_pair_half(1, below, 1, 7)
+        ring_wait(above, 0, 2)
+        to_pair_half(-1, above, 0, 9)
+        to_sibling(ring.at[below], below, 1)
+        to_sibling(ring.at[above], above, 2)
 
     def far_shard():
         ring_wait(quarters[2], 0, 4)
@@ -193,16 +203,16 @@
             lower = height[4 * j + 2] + height[4 * j + 3]
             sq_v[pl.ds(64 * f, 64), 128 * j : 128 * j + 128] = jnp.where(low, upper, lower).astype(BF)
 
-    hear_news(0)
-    spread_news(1)
     loads[2].wait()
     for f in range(2):
         sums = dot(x_v[f].reshape(1024, 128), pairs)
         for b in range(3):
             pool[1 + b, pl.ds(f * 1024, 1024), :] = sums[:, 128 * b : 128 * b + 128]
+    hear_news(0)
+    spread_news(1)
+    near_shards()
     hear_news(1)
     spread_news(2)
-    near_shards()
     for f in range(2):
         for b in range(3):
             height = [pool[1 + b, pl.ds(f * 1024 + h, 64, stride=16), :] for h in range(16)]
@@ -356,6 +366,8 @@
         for offset in FAR_FIRST:
             src = gr_v.at[here]
             remote(src, src, ag_send, ag_recv, (2 * chip_at(offset) + core, c)).start()
+            remote(src, src, sib_send, sib_recv, (2 * chip_at(offset) + 1 - core, c)).start()
+        remote(src, src, sib_send, sib_recv, sibling).start()
 
     @pl.when(large)
     def _():
@@ -381,9 +393,8 @@
     def _():
         rest(PIECES - 1, ag_recv)
 
-    mine = pl.ds(core * PIECES, PIECES)
-    handover = remote(gr_v.at[mine], gr_v.at[mine], sib_send, sib_recv, sibling)
-    handover.start()
+
+    rest(PIECES, sib_recv)
 
     for copy in sent:
         copy.wait_send()
@@ -399,13 +410,13 @@
     def _():
         rest(PIECES - 2, rs_send)
         rest(2 * (CHIPS - 1), ag_send)
+        rest(2 * CHIPS, sib_send)
 
     @pl.when(jnp.logical_not(large))
     def _():
         rest(PIECES - 1, rs_send)
         rest(CHIPS - 1, ag_send)
-
-    handover.wait()
+        rest(CHIPS, sib_send)
 
 
 def finish(ig_v, gr_v, ig_out, sp_out, te_out, wide_v, sem):
@@ -463,7 +474,7 @@
             dma((5,)),
             dma((6,)),
             dma((6,)),
-            dma((8,)),
+            dma((10,)),
             dma((2,)),
             dma, dma,
             dma, dma,

time: 36.5 us -> 35.8 us (0.981)
  Pallas kernels: 35.7 us -> 35 us
    pallas_call x1, Pallas kernels: 34.7 us -> 33.9 us  [shards(): pl.pallas_call(kernel, out_shape=(pltpu.VMEM((2, 64, 16, 128), BF), pltpu...]
where the time goes in v4:
time: 35.8 us; the launch traced here: 35.7 us
  Pallas kernels  35 us (98%)
  between operations  0.64 us (2%)
    pallas_call x1, Pallas kernels, shards(): pl.pallas_call(kernel, out_shape=(pltpu.VMEM((2, 64, 16, 128), BF), pltpu...  33.9 us
    pallas_call x1, Pallas kernels, shards(): pl.pallas_call(finish, out_shape=(jax.ShapeDtypeStruct((2, 64, 16, 128),...  1.09 us

profile of v4, /device:TPU:1, one launch (start us, length us, event | category | flops | bytes accessed | tf_op | source)
XLA Modules:
  0.0 35.7 jit_solution(11345322579469607088)
XLA Ops:
  0.6 33.9 %space_time_backward.1 = (bf16[2,64,16,128]{3,2,1,0:T(8,128)(2,1)S(1)}, bf16[96,16,128]{2,1,0:T(8,128)(2,1)S(1)}) custom-call(bf16[2,64,16,128]{3,2,1,0:T(8,128)(2,1)} %x_h.1, bf16[2,64,16,128]{3,2,1,0:T(8,128)(2,1)} %s_h.1, bf16[1,64,512]{2,1,0:T(8,128)(2,1)} %c_h.1, bf16[3,3,64,256]{3,2,1,0:T(8,128)(2,1)} %sw_h.1, bf16[3,256,256]{2,1,0:T(8,128)(2,1)} %tw_h.1), custom_call_target="tpu_custom_call" | custom-call | tf_op jit(solution)/shard_map/space_time_backward/pallas_call | solution.py:443
  34.6 1.1 %scale_gradients.1 = (bf16[2,64,16,128]{3,2,1,0:T(8,128)(2,1)}, f32[36,16,256]{2,1,0:T(8,128)}, f32[12,16,256]{2,1,0:T(8,128)}) custom-call(bf16[2,64,16,128]{3,2,1,0:T(8,128)(2,1)S(1)} %get-tuple-element.8.ig_v, bf16[96,16,128]{2,1,0:T(8,128)(2,1)S(1)} %get-tuple-element.9.gr_v), custom_call_target="tpu_custom_call" | custom-call | tf_op jit(solution)/shard_map/scale_gradients/pallas_call | solution.py:492

commit v5 on v4

--- a/solution.py
+++ b/solution.py
@@ -37,7 +37,7 @@
     x_v, s_v, sw_v, tw_v, ring, halo, pool, q_v, sq_v, a_v, g_v, p_v, xe_v, z_v,
     given, kept, xch, half_v, rs_v,
     load_sem, ring_send_sem, ring_recv, fwd_send, halo_recv,
-    xch_send, xch_recv, rs_send, rs_recv, ag_send, ag_recv, sib_send, sib_recv, news,
+    xch_send, xch_recv, rs_send, rs_recv, ag_send, ag_recv, news,
 ):
     p = lax.axis_index("frames")
     c = lax.axis_index("chan")
@@ -363,11 +363,21 @@
             total = total + rs_v[count * slot : count * slot + count].astype(F32)
         here = pl.ds(core * PIECES + at, count)
         gr_v[here] = total.astype(BF)
-        for offset in FAR_FIRST:
-            src = gr_v.at[here]
-            remote(src, src, ag_send, ag_recv, (2 * chip_at(offset) + core, c)).start()
-            remote(src, src, sib_send, sib_recv, (2 * chip_at(offset) + 1 - core, c)).start()
-        remote(src, src, sib_send, sib_recv, sibling).start()
+        src = gr_v.at[here]
+
+        def hand_out(target):
+            for side in (1, 0):
+                remote(src, src, ag_send.at[side], ag_recv.at[core], (2 * target + side, c)).start()
+
+        remote(src, src, ag_send.at[1 - core], ag_recv.at[core], sibling).start()
+
+        for i, j, k in [(0, 0, 0)] + FAR_FIRST[::-1]:
+            target = 8 * i + 2 * j + k
+
+            @pl.when(target != chip)
+            def _():
+                hand_out(target)
+
 
     @pl.when(large)
     def _():
@@ -387,14 +397,14 @@
 
     @pl.when(large)
     def _():
-        rest(PIECES - 2, ag_recv)
+        rest(PIECES - 2, ag_recv.at[core])
 
     @pl.when(jnp.logical_not(large))
     def _():
-        rest(PIECES - 1, ag_recv)
-
-
-    rest(PIECES, sib_recv)
+        rest(PIECES - 1, ag_recv.at[core])
+
+
+    rest(PIECES, ag_recv.at[1 - core])
 
     for copy in sent:
         copy.wait_send()
@@ -409,14 +419,14 @@
     @pl.when(large)
     def _():
         rest(PIECES - 2, rs_send)
-        rest(2 * (CHIPS - 1), ag_send)
-        rest(2 * CHIPS, sib_send)
+        rest(2 * (CHIPS - 1), ag_send.at[core])
+        rest(2 * CHIPS, ag_send.at[1 - core])
 
     @pl.when(jnp.logical_not(large))
     def _():
         rest(PIECES - 1, rs_send)
-        rest(CHIPS - 1, ag_send)
-        rest(CHIPS, sib_send)
+        rest(CHIPS - 1, ag_send.at[core])
+        rest(CHIPS, ag_send.at[1 - core])
 
 
 def finish(ig_v, gr_v, ig_out, sp_out, te_out, wide_v, sem):
@@ -478,8 +488,7 @@
             dma((2,)),
             dma, dma,
             dma, dma,
-            dma, dma,
-            dma, dma,
+            dma((2,)), dma((2,)),
             pltpu.SemaphoreType.REGULAR((ROUNDS,)),
         ],
         compiler_params=pltpu.CompilerParams(

time: 35.8 us -> 35.3 us (0.986)
  Pallas kernels: 35 us -> 34.6 us
    pallas_call x1, Pallas kernels: 33.9 us -> 33.5 us  [shards(): pl.pallas_call(kernel, out_shape=(pltpu.VMEM((2, 64, 16, 128), BF), pltpu...]
where the time goes in v5:
time: 35.3 us; the launch traced here: 35.2 us
  Pallas kernels  34.6 us (98%)
  between operations  0.64 us (2%)
    pallas_call x1, Pallas kernels, shards(): pl.pallas_call(kernel, out_shape=(pltpu.VMEM((2, 64, 16, 128), BF), pltpu...  33.5 us
    pallas_call x1, Pallas kernels, shards(): pl.pallas_call(finish, out_shape=(jax.ShapeDtypeStruct((2, 64, 16, 128),...  1.09 us

profile of v5, /device:TPU:1, one launch (start us, length us, event | category | flops | bytes accessed | tf_op | source)
XLA Modules:
  0.0 35.2 jit_solution(7952182368091410576)
XLA Ops:
  0.6 33.5 %space_time_backward.1 = (bf16[2,64,16,128]{3,2,1,0:T(8,128)(2,1)S(1)}, bf16[96,16,128]{2,1,0:T(8,128)(2,1)S(1)}) custom-call(bf16[2,64,16,128]{3,2,1,0:T(8,128)(2,1)} %x_h.1, bf16[2,64,16,128]{3,2,1,0:T(8,128)(2,1)} %s_h.1, bf16[1,64,512]{2,1,0:T(8,128)(2,1)} %c_h.1, bf16[3,3,64,256]{3,2,1,0:T(8,128)(2,1)} %sw_h.1, bf16[3,256,256]{2,1,0:T(8,128)(2,1)} %tw_h.1), custom_call_target="tpu_custom_call" | custom-call | tf_op jit(solution)/shard_map/space_time_backward/pallas_call | solution.py:453
  34.1 1.1 %scale_gradients.1 = (bf16[2,64,16,128]{3,2,1,0:T(8,128)(2,1)}, f32[36,16,256]{2,1,0:T(8,128)}, f32[12,16,256]{2,1,0:T(8,128)}) custom-call(bf16[2,64,16,128]{3,2,1,0:T(8,128)(2,1)S(1)} %get-tuple-element.8.ig_v, bf16[96,16,128]{2,1,0:T(8,128)(2,1)S(1)} %get-tuple-element.9.gr_v), custom_call_target="tpu_custom_call" | custom-call | tf_op jit(solution)/shard_map/scale_gradients/pallas_call | solution.py:501

commit v6 on v5

--- a/solution.py
+++ b/solution.py
@@ -10,6 +10,7 @@
 BF = jnp.bfloat16
 F32 = jnp.float32
 CHIPS = 32
+PARTS = 2
 PIECES = 48
 
 
@@ -103,21 +104,21 @@
 
     sent = []
 
-    def rows(half):
-        return pl.ds(32 * half, 32)
+    def rows(part):
+        return pl.ds(64 // PARTS * part, 64 // PARTS)
 
     quarters = {step: lax.rem(c + step + 4, 4) for step in (-1, 0, 1, 2)}
 
-    def ring_send(hop, quarter, half, index, src=None):
+    def ring_send(hop, quarter, part, index, src=None):
         copy = remote(
-            ring.at[quarter, rows(half)] if src is None else src, ring.at[quarter, rows(half)],
+            ring.at[quarter, rows(part)] if src is None else src, ring.at[quarter, rows(part)],
             ring_send_sem.at[index], ring_recv.at[index], in_ring(hop),
         )
         copy.start()
         sent.append(copy)
 
-    def ring_wait(quarter, half, index):
-        dst = ring.at[quarter, rows(half)]
+    def ring_wait(quarter, part, index):
+        dst = ring.at[quarter, rows(part)]
         remote(dst, dst, ring_send_sem.at[index], ring_recv.at[index], sibling).wait_recv()
 
     def to_sibling(src, quarter, index):
@@ -139,37 +140,37 @@
 
         pair_copies.append(copy)
 
-    def to_pair_half(step, quarter, half, index):
+    def to_pair_part(step, quarter, part, index):
         to_pair(
-            step, ring.at[quarter, rows(half)], quarter, index,
-            halo.at[1 - core, quarter, rows(half)],
+            step, ring.at[quarter, rows(part)], quarter, index,
+            halo.at[1 - core, quarter, rows(part)],
         )
 
-    for half in range(2):
-        ring_send(2, c, half, half, ring.at[c, rows(half)])
-        ring_send(-2, c, 1 - half, 3 - half, ring.at[c, rows(1 - half)])
+    for part in range(PARTS):
+        ring_send(2, c, part, part, ring.at[c, rows(part)])
+        ring_send(-2, c, PARTS - 1 - part, 2 * PARTS - 1 - part, ring.at[c, rows(PARTS - 1 - part)])
     to_pair(1, ring.at[c], c, 4)
     to_pair(-1, ring.at[c], c, 5)
     to_sibling(ring.at[c], c, 0)
 
     def near_shards():
         below, above = quarters[-1], quarters[1]
-        ring_wait(below, 0, 0)
-        ring_send(2, below, 0, 4)
-        ring_wait(above, 1, 3)
-        ring_send(-2, above, 1, 5)
-        to_pair_half(1, below, 0, 6)
-        to_pair_half(-1, above, 1, 8)
-        ring_wait(below, 1, 1)
-        to_pair_half(1, below, 1, 7)
-        ring_wait(above, 0, 2)
-        to_pair_half(-1, above, 0, 9)
+        for part in range(PARTS):
+            last = PARTS - 1 - part
+            ring_wait(below, part, part)
+            if part < PARTS // 2:
+                ring_send(2, below, part, 2 * PARTS + part)
+            ring_wait(above, last, PARTS + last)
+            if part < PARTS // 2:
+                ring_send(-2, above, last, 2 * PARTS + last)
+            to_pair_part(1, below, part, 6 + part)
+            to_pair_part(-1, above, last, 6 + PARTS + last)
         to_sibling(ring.at[below], below, 1)
         to_sibling(ring.at[above], above, 2)
 
     def far_shard():
-        ring_wait(quarters[2], 0, 4)
-        ring_wait(quarters[2], 1, 5)
+        for part in range(PARTS):
+            ring_wait(quarters[2], part, 2 * PARTS + part)
         to_sibling(ring.at[quarters[2]], quarters[2], 3)
 
     def spread_news(k):
@@ -230,7 +231,9 @@
     far_shard()
 
     own = ring[...].reshape(256, 512)
-    a_v[...] = dot(tw_v[...].reshape(768, 256), own)
+    taps = dot(tw_v[...].reshape(768, 256), own)
+    a_v[0] = taps[0:256] + taps[256:512]
+    a_v[1] = taps[256:512] + taps[512:768]
     t_own = dot_nt(sq_v[...], own)
 
     dst = halo.at[1 - core]
@@ -247,9 +250,8 @@
 
     before = halo[0].reshape(256, 512)
     after = halo[1].reshape(256, 512)
-    middle = a_v[256:512]
-    g_v[0] = ((a_v[0:256] + middle + dot(tw_v[2], before)) * 0.125).astype(BF)
-    g_v[1] = ((dot(tw_v[0], after) + middle + a_v[512:768]) * 0.125).astype(BF)
+    g_v[0] = ((a_v[0] + dot(tw_v[2], before)) * 0.125).astype(BF)
+    g_v[1] = ((a_v[1] + dot(tw_v[0], after)) * 0.125).astype(BF)
 
     def put(dst, at, value):
         count = value.shape[0] // 16
@@ -322,7 +324,7 @@
                 for k in range(2):
                     h = 2 * (2 * j + k) + r
                     z_v[pl.ds(h, 64, stride=16), :] = woven[r, j, :, 128 * k : 128 * k + 128]
-        ig_v[f] = z_v[...].reshape(64, 16, 128).astype(BF)
+        ig_v[f] = z_v[0:1024].reshape(64, 16, 128).astype(BF)
 
     exchange.wait_recv()
     half_v[...] = (kept[...] + xch[...].astype(F32)).astype(BF).reshape(PIECES, 16, 128)
@@ -468,23 +470,23 @@
             vmem((3, 256, 256), BF),
             vmem((4, 64, 512), BF),
             vmem((2, 4, 64, 512), BF),
-            vmem((4, 2048, 128), F32),
+            vmem((4, 2048 + 16, 128), F32),
             vmem((2, 576, 512), BF),
             vmem((128, 512), BF),
-            vmem((768, 512), F32),
+            vmem((2, 256, 512), F32),
             vmem((2, 256, 512), BF),
             vmem((9, 64, 512), F32),
             vmem((2, 4, 64, 256), BF),
-            vmem((1024, 128), F32),
+            vmem((1024 + 16, 128), F32),
             vmem((24, 2, 16, 128), BF),
             vmem((24, 2, 16, 128), F32),
             vmem((24, 2, 16, 128), BF),
             vmem((PIECES, 16, 128), BF),
             vmem((2 * (CHIPS - 1), 16, 128), BF),
             dma((5,)),
-            dma((6,)),
-            dma((6,)),
-            dma((10,)),
+            dma((3 * PARTS,)),
+            dma((3 * PARTS,)),
+            dma((6 + 2 * PARTS,)),
             dma((2,)),
             dma, dma,
             dma, dma,

time: 35.3 us -> 35.3 us (level)
  no operation moved by 1% of the time
where the time goes in v6:
time: 35.3 us
  Pallas kernels  34.6 us (98%)
  between operations  0.64 us (2%)
    pallas_call x1, Pallas kernels, shards(): pl.pallas_call(kernel, out_shape=(pltpu.VMEM((2, 64, 16, 128), BF), pltpu...  33.5 us
    pallas_call x1, Pallas kernels, shards(): pl.pallas_call(finish, out_shape=(jax.ShapeDtypeStruct((2, 64, 16, 128),...  1.09 us

profile of v6, /device:TPU:1, one launch (start us, length us, event | category | flops | bytes accessed | tf_op | source)
XLA Modules:
  0.0 35.3 jit_solution(7674857540538022470)
XLA Ops:
  0.6 33.5 %space_time_backward.1 = (bf16[2,64,16,128]{3,2,1,0:T(8,128)(2,1)S(1)}, bf16[96,16,128]{2,1,0:T(8,128)(2,1)S(1)}) custom-call(bf16[2,64,16,128]{3,2,1,0:T(8,128)(2,1)} %x_h.1, bf16[2,64,16,128]{3,2,1,0:T(8,128)(2,1)} %s_h.1, bf16[1,64,512]{2,1,0:T(8,128)(2,1)} %c_h.1, bf16[3,3,64,256]{3,2,1,0:T(8,128)(2,1)} %sw_h.1, bf16[3,256,256]{2,1,0:T(8,128)(2,1)} %tw_h.1), custom_call_target="tpu_custom_call" | custom-call | tf_op jit(solution)/shard_map/space_time_backward/pallas_call | solution.py:455
  34.2 1.1 %scale_gradients.1 = (bf16[2,64,16,128]{3,2,1,0:T(8,128)(2,1)}, f32[36,16,256]{2,1,0:T(8,128)}, f32[12,16,256]{2,1,0:T(8,128)}) custom-call(bf16[2,64,16,128]{3,2,1,0:T(8,128)(2,1)S(1)} %get-tuple-element.8.ig_v, bf16[96,16,128]{2,1,0:T(8,128)(2,1)S(1)} %get-tuple-element.9.gr_v), custom_call_target="tpu_custom_call" | custom-call | tf_op jit(solution)/shard_map/scale_gradients/pallas_call | solution.py:503

commit v7 on v6

--- a/solution.py
+++ b/solution.py
@@ -16,7 +16,7 @@
 
 FAR_FIRST = sorted(
     [(i, j, k) for i in range(4) for j in range(4) for k in range(2) if i or j or k],
-    key=lambda s: -(min(s[0], 4 - s[0]) + min(s[1], 4 - s[1]) + s[2]),
+    key=lambda s: (-(min(s[0], 4 - s[0]) + min(s[1], 4 - s[1]) + s[2]), s[2], s[0] + s[1]),
 )
 
 

time: 35.3 us -> 35.3 us (level)
  no operation moved by 1% of the time
where the time goes in v7:
time: 35.3 us; the launch traced here: 35.2 us
  Pallas kernels  34.6 us (98%)
  between operations  0.64 us (2%)
    pallas_call x1, Pallas kernels, shards(): pl.pallas_call(kernel, out_shape=(pltpu.VMEM((2, 64, 16, 128), BF), pltpu...  33.5 us
    pallas_call x1, Pallas kernels, shards(): pl.pallas_call(finish, out_shape=(jax.ShapeDtypeStruct((2, 64, 16, 128),...  1.09 us

profile of v7, /device:TPU:1, one launch (start us, length us, event | category | flops | bytes accessed | tf_op | source)
XLA Modules:
  0.0 35.2 jit_solution(17601136097128356995)
XLA Ops:
  0.6 33.5 %space_time_backward.1 = (bf16[2,64,16,128]{3,2,1,0:T(8,128)(2,1)S(1)}, bf16[96,16,128]{2,1,0:T(8,128)(2,1)S(1)}) custom-call(bf16[2,64,16,128]{3,2,1,0:T(8,128)(2,1)} %x_h.1, bf16[2,64,16,128]{3,2,1,0:T(8,128)(2,1)} %s_h.1, bf16[1,64,512]{2,1,0:T(8,128)(2,1)} %c_h.1, bf16[3,3,64,256]{3,2,1,0:T(8,128)(2,1)} %sw_h.1, bf16[3,256,256]{2,1,0:T(8,128)(2,1)} %tw_h.1), custom_call_target="tpu_custom_call" | custom-call | tf_op jit(solution)/shard_map/space_time_backward/pallas_call | solution.py:455
  34.1 1.1 %scale_gradients.1 = (bf16[2,64,16,128]{3,2,1,0:T(8,128)(2,1)}, f32[36,16,256]{2,1,0:T(8,128)}, f32[12,16,256]{2,1,0:T(8,128)}) custom-call(bf16[2,64,16,128]{3,2,1,0:T(8,128)(2,1)S(1)} %get-tuple-element.8.ig_v, bf16[96,16,128]{2,1,0:T(8,128)(2,1)S(1)} %get-tuple-element.9.gr_v), custom_call_target="tpu_custom_call" | custom-call | tf_op jit(solution)/shard_map/scale_gradients/pallas_call | solution.py:503

commit v8 on v7

--- a/solution.py
+++ b/solution.py
@@ -433,16 +433,16 @@
 
 def finish(ig_v, gr_v, ig_out, sp_out, te_out, wide_v, sem):
     scale = 1.0 / math.sqrt(128 * 16 * 128)
-    stores = [pltpu.make_async_copy(ig_v, ig_out, sem.at[4])]
+    stores = [pltpu.make_async_copy(ig_v, ig_out, sem.at[8])]
     stores[0].start()
-    for k in range(4):
-        pieces = gr_v[24 * k : 24 * k + 24].reshape(12, 2, 16, 128)
+    for k in range(8):
+        pieces = gr_v[12 * k : 12 * k + 12].reshape(6, 2, 16, 128)
         for side in range(2):
-            wide_v[12 * k : 12 * k + 12, :, 128 * side : 128 * side + 128] = (
+            wide_v[6 * k : 6 * k + 6, :, 128 * side : 128 * side + 128] = (
                 pieces[:, side].astype(F32) * scale
             )
-        dst = te_out if k == 0 else sp_out.at[pl.ds(12 * k - 12, 12)]
-        store = pltpu.make_async_copy(wide_v.at[pl.ds(12 * k, 12)], dst, sem.at[k])
+        dst = te_out.at[pl.ds(6 * k, 6)] if k < 2 else sp_out.at[pl.ds(6 * k - 12, 6)]
+        store = pltpu.make_async_copy(wide_v.at[pl.ds(6 * k, 6)], dst, sem.at[k])
         store.start()
         stores.append(store)
     for store in stores:
@@ -511,7 +511,7 @@
         out_specs=[pl.BlockSpec(memory_space=pl.ANY)] * 3,
         scratch_shapes=[
             vmem((48, 16, 256), F32),
-            dma((5,)),
+            dma((9,)),
         ],
         name="scale_gradients",
     )(input_grad, grads)

time: 35.3 us -> 35.3 us (level)
  no operation moved by 1% of the time
where the time goes in v8:
time: 35.3 us; the launch traced here: 35.2 us
  Pallas kernels  34.6 us (98%)
  between operations  0.64 us (2%)
    pallas_call x1, Pallas kernels, shards(): pl.pallas_call(kernel, out_shape=(pltpu.VMEM((2, 64, 16, 128), BF), pltpu...  33.5 us
    pallas_call x1, Pallas kernels, shards(): pl.pallas_call(finish, out_shape=(jax.ShapeDtypeStruct((2, 64, 16, 128),...  1.12 us

profile of v8, /device:TPU:1, one launch (start us, length us, event | category | flops | bytes accessed | tf_op | source)
XLA Modules:
  0.0 35.2 jit_solution(6841609575353838235)
XLA Ops:
  0.6 33.5 %space_time_backward.1 = (bf16[2,64,16,128]{3,2,1,0:T(8,128)(2,1)S(1)}, bf16[96,16,128]{2,1,0:T(8,128)(2,1)S(1)}) custom-call(bf16[2,64,16,128]{3,2,1,0:T(8,128)(2,1)} %x_h.1, bf16[2,64,16,128]{3,2,1,0:T(8,128)(2,1)} %s_h.1, bf16[1,64,512]{2,1,0:T(8,128)(2,1)} %c_h.1, bf16[3,3,64,256]{3,2,1,0:T(8,128)(2,1)} %sw_h.1, bf16[3,256,256]{2,1,0:T(8,128)(2,1)} %tw_h.1), custom_call_target="tpu_custom_call" | custom-call | tf_op jit(solution)/shard_map/space_time_backward/pallas_call | solution.py:455
  34.1 1.1 %scale_gradients.1 = (bf16[2,64,16,128]{3,2,1,0:T(8,128)(2,1)}, f32[36,16,256]{2,1,0:T(8,128)}, f32[12,16,256]{2,1,0:T(8,128)}) custom-call(bf16[2,64,16,128]{3,2,1,0:T(8,128)(2,1)S(1)} %get-tuple-element.8.ig_v, bf16[96,16,128]{2,1,0:T(8,128)(2,1)S(1)} %get-tuple-element.9.gr_v), custom_call_target="tpu_custom_call" | custom-call | tf_op jit(solution)/shard_map/scale_gradients/pallas_call | solution.py:503
